TPU v7x, 256 devices: a whole 4x4x8 slice. The times are simulated.
256 devices in a mesh: row: 16 (over z, core), col: 16 (over y, x).
Axes of the slice: x: 4, y: 4, z: 8, core: 2. Of those that a mesh axis runs over, the one named last changes fastest.
Arguments:
- embed: bfloat16 [8192, 1024], P(('row', 'col')), may hold values from -0.1875 to 0.1875
- positives: int32 [8192, 4], P('row'), may hold values from 0 to 8191, as said below
- placement: int32 [8192], replicated, may hold values from 0 to 8191, as said below
Outputs:
- embed_grad: float32 [8192, 1024], P(('row', 'col'))
Inputs may be any that keep to these rules, and one draw needn't show every extreme that they name: `positives`: each row names 4 different entities, none of them the entity placed at that row's position. `placement`: a permutation of the entity ids.
All inputs are finite; a program needn't handle non-finite values.
Results may differ from a plain program's by a relative error of at most 0.003.
Values may be sent and summed in bfloat16 or wider, within the bound.
A program may use at most 64 MiB of HBM per device.

v0:
```python
import jax
import jax.numpy as jnp
from jax import lax
from jax.sharding import PartitionSpec as P

logistic_sharpness = 0.02


def positive_rank(matching_pair_affinity_lines):
    affinity_differences = (
        matching_pair_affinity_lines[:, None, :] - matching_pair_affinity_lines[:, :, None]
    ) / logistic_sharpness
    return 0.5 + jnp.sum(jax.nn.sigmoid(affinity_differences), axis=2)


def coefficients(matching_pair_affinity_lines, ranks, slopes, total):
    prank, pullback = jax.vjp(positive_rank, matching_pair_affinity_lines)
    factor = 1.0 / (matching_pair_affinity_lines.shape[1] * total)
    smoothed_ordering_slope = prank / (ranks * ranks) * factor
    prank_grad = -factor / ranks
    pulled = pullback(prank_grad)[0]
    ordering_coefficient_vector = smoothed_ordering_slope / logistic_sharpness
    extra = pulled - ordering_coefficient_vector * slopes
    return (ordering_coefficient_vector, extra)


def sigmoid_sums(cosine_affinity_matrix, matching_pair_affinity_lines, allowed):
    counts = []
    slopes = []
    for element_location in range(matching_pair_affinity_lines.shape[1]):
        difference_before_squash = jax.nn.sigmoid(
            (
                cosine_affinity_matrix
                - matching_pair_affinity_lines[:, element_location : element_location + 1]
            )
            / logistic_sharpness
        )
        counts.append(jnp.sum(jnp.where(allowed, difference_before_squash, 0.0), axis=1))
        slopes.append(
            jnp.sum(
                jnp.where(
                    allowed, difference_before_squash * (1.0 - difference_before_squash), 0.0
                ),
                axis=1,
            )
        )
    return (jnp.stack(counts, axis=1), jnp.stack(slopes, axis=1))


def score_grads(
    cosine_affinity_matrix,
    matching_pair_affinity_lines,
    allowed,
    column_pos,
    targets,
    ordering_coefficient_vector,
    extra,
):
    dense = jnp.zeros(cosine_affinity_matrix.shape, jnp.float32)
    for element_location in range(matching_pair_affinity_lines.shape[1]):
        difference_before_squash = jax.nn.sigmoid(
            (
                cosine_affinity_matrix
                - matching_pair_affinity_lines[:, element_location : element_location + 1]
            )
            / logistic_sharpness
        )
        dense = dense + ordering_coefficient_vector[
            :, element_location : element_location + 1
        ] * jnp.where(allowed, difference_before_squash * (1.0 - difference_before_squash), 0.0)
    for element_location in range(matching_pair_affinity_lines.shape[1]):
        dense = dense + jnp.where(
            column_pos[None, :] == targets[:, element_location : element_location + 1],
            extra[:, element_location : element_location + 1],
            0.0,
        )
    return dense.astype(jnp.bfloat16)


def body(embed, positives, placement):
    shard = embed.shape[0]
    row_count = lax.axis_size("row")
    col_count = lax.axis_size("col")
    total = shard * row_count * col_count
    row_id = lax.axis_index("row")
    col_id = lax.axis_index("col")
    anchors = lax.all_gather(embed, "col", axis=0, tiled=True)
    candidates = lax.all_gather(embed, "row", axis=0, tiled=True)
    anchor_width = anchors.shape[0]
    targets = jnp.take(placement, positives)
    own = row_id * anchor_width + jnp.arange(anchor_width, dtype=jnp.int32)
    local = jnp.arange(candidates.shape[0], dtype=jnp.int32)
    column_pos = local // shard * anchor_width + col_id * shard + local % shard
    allowed = column_pos[None, :] != own[:, None]
    cosine_affinity_matrix = jnp.einsum(
        "ad,kd->ak", anchors, candidates, preferred_element_type=jnp.float32
    )
    columns = []
    for element_location in range(targets.shape[1]):
        found = column_pos[None, :] == targets[:, element_location : element_location + 1]
        columns.append(jnp.sum(jnp.where(found, cosine_affinity_matrix, 0.0), axis=1))
    pos_part = jnp.stack(columns, axis=1)
    matching_pair_affinity_lines = lax.psum(pos_part, "col")
    count_part, slope_part = sigmoid_sums(
        cosine_affinity_matrix, matching_pair_affinity_lines, allowed
    )
    count_sum, slope_sum = lax.psum((count_part, slope_part), "col")
    ordering_coefficient_vector, extra = coefficients(
        matching_pair_affinity_lines, 0.5 + count_sum, slope_sum, total
    )
    grad_tile = score_grads(
        cosine_affinity_matrix,
        matching_pair_affinity_lines,
        allowed,
        column_pos,
        targets,
        ordering_coefficient_vector,
        extra,
    )
    part = grad_tile
    grad_anchor = lax.psum_scatter(
        jnp.dot(part, candidates, preferred_element_type=jnp.float32),
        "col",
        scatter_dimension=0,
        tiled=True,
    )
    part = grad_tile
    grad_candidate = lax.psum_scatter(
        lax.dot_general(
            part, anchors, (((0,), (0,)), ((), ())), preferred_element_type=jnp.float32
        ),
        "row",
        scatter_dimension=0,
        tiled=True,
    )
    return grad_anchor + grad_candidate


def solution(mesh):
    return jax.shard_map(
        body,
        mesh=mesh,
        in_specs=(P(("row", "col"), None), P("row", None), P()),
        out_specs=P(("row", "col"), None),
        check_vma=False,
    )
```

profile of v0, /device:TPU:1, one launch (start us, length us, event | category | flops | bytes accessed | tf_op | source)
XLA Modules:
  0.0 361.8 jit_solution(211732697152032881)
XLA Ops:
  6.5 0.0 copy-start
  6.5 0.0 all-gather.3.cloned.1.call-start
  6.5 0.7 all-gather.3.cloned.1.call-update
  7.3 0.0 all-gather.5.cloned.1.call-start
  7.3 0.7 all-gather.5.cloned.1.call-update
  8.0 0.0 reduce-scatter.5.cloned.1.call-start
  8.1 0.7 compare_select_fusion.16
  8.8 0.1 copy.25
  8.9 0.2 reshape.42
  9.1 0.0 copy-done
  9.1 0.0 copy-start.3
  9.1 11.8 %gather_fusion = s32[2048]{0:T(1024)S(1)} fusion(s32[8192]{0:T(1024)S(1)} %copy-done, s32[2048]{0:T(1024)S(1)} %broadcast_clamp_fusion), kind=kCustom, calls=%fused_computation | custom fusion | bytes 24576 | tf_op jit(solution)/shard_map/jit(_take)/gather | solution.py:90
  20.9 0.3 reshape.41
  21.2 0.1 copy.26
  21.3 0.0 copy-done.3
  21.3 38.6 %all-gather.3.cloned.1.call-done = bf16[512,1024]{1,0:T(8,128)(2,1)} async-done(((bf16[32,1024]{1,0:T(8,128)(2,1)}), bf16[512,1024]{1,0:T(8,128)(2,1)}) %all-gather.3.cloned.1.call-update) | async-done | bytes 1048592 | tf_op jit(solution)/shard_map/all_gather | solution.py:87
  59.9 41.6 %all-gather.5.cloned.1.call-done = bf16[512,1024]{1,0:T(8,128)(2,1)} async-done(((bf16[32,1024]{1,0:T(8,128)(2,1)}), bf16[512,1024]{1,0:T(8,128)(2,1)}) %all-gather.5.cloned.1.call-update) | async-done | bytes 1048592 | tf_op jit(solution)/shard_map/all_gather | solution.py:88
  101.5 2.6 fusion
  104.1 33.7 %psum.21 = f32[512,4]{0,1:T(4,128)S(1)} all-reduce(f32[512,4]{0,1:T(4,128)S(1)} %pad_maximum_fusion), channel_id=1, replica_groups=mesh['row'=16,'col'=16] {'col'}, use_global_device_ids=true, to_apply=%region_4.5 | all-reduce | flops 2048 | bytes 16384 | tf_op jit(solution)/shard_map/psum | solution.py:103
  137.8 0.0 copy-start.2
  137.8 2.0 fusion.13
  139.9 56.1 %all-reduce = (f32[512,4]{0,1:T(4,128)S(1)}, f32[512,4]{0,1:T(4,128)S(1)}) all-reduce(f32[512,4]{0,1:T(4,128)S(1)} %pad_maximum_fusion.1, f32[512,4]{0,1:T(4,128)S(1)} %pad_maximum_fusion.2), channel_id=1, replica_groups=mesh['row'=16,'col'=16] {'col'}, use_global_device_ids=true, to_apply=%region_10.11 | all-reduce | flops 4096 | bytes 32768 | tf_op jit(solution)/shard_map/psum | solution.py:107
  196.0 0.1 fusion.20
  196.1 2.2 fusion.5
  198.3 2.1 fusion.39
  200.4 0.0 reduce-scatter.5.cloned.1.call-update
  200.4 0.0 reduce-scatter.3.cloned.1.call-start
  200.5 2.0 fusion.38
  202.5 0.0 reduce-scatter.3.cloned.1.call-update
  202.5 68.4 %reduce-scatter.5.cloned.1.call-done = f32[32,1024]{1,0:T(8,128)} async-done(((f32[512,1024]{1,0:T(8,128)}), f32[32,1024]{1,0:T(8,128)}) %reduce-scatter.5.cloned.1.call-update) | async-done | bytes 131088 | tf_op jit(solution)/shard_map/reduce_scatter | solution.py:128
  270.9 82.7 %reduce-scatter.3.cloned.1.call-done = f32[32,1024]{1,0:T(8,128)} async-done(((f32[512,1024]{1,0:T(8,128)}), f32[32,1024]{1,0:T(8,128)}) %reduce-scatter.3.cloned.1.call-update) | async-done | bytes 131088 | tf_op jit(solution)/shard_map/reduce_scatter | solution.py:121
  353.6 1.6 add.131
  (15 shorter events, 0.1 us)
Async XLA Ops:
  6.5 2.6 copy-start
  6.5 53.4 %all-gather.3.cloned.1.call-start = ((), (), s32[]{:S(2)}) async-start(), calls=%async_computation.2 | async-start | bytes 1114112 | tf_op jit(solution)/shard_map/all_gather | solution.py:87
  7.3 94.2 %all-gather.5.cloned.1.call-start = ((), (), s32[]{:S(2)}) async-start(), calls=%async_computation.3 | async-start | bytes 1114112 | tf_op jit(solution)/shard_map/all_gather | solution.py:88
  8.0 262.9 %reduce-scatter.5.cloned.1.call-start = ((), (), s32[]{:S(2)}) async-start(), calls=%async_computation.5 | async-start | bytes 2228224 | tf_op jit(solution)/shard_map/reduce_scatter | solution.py:128
  9.1 12.2 %copy-start.3 = (s32[512,4]{0,1:T(4,128)S(1)}, s32[512,4]{0,1:T(4,128)}, u32[]{:S(2)}) copy-start(s32[512,4]{0,1:T(4,128)} %param.4) | copy-start | bytes 24580
  137.8 60.5 %copy-start.2 = (bf16[512,1024]{1,0:T(8,128)(2,1)S(1)}, bf16[512,1024]{1,0:T(8,128)(2,1)}, u32[]{:S(2)}) copy-start(bf16[512,1024]{1,0:T(8,128)(2,1)} %all-gather.3.cloned.1.call-done) | copy-start | bytes 3145732
  198.3 2.2 copy-start.1
  200.4 153.2 %reduce-scatter.3.cloned.1.call-start = ((), (), s32[]{:S(2)}) async-start(), calls=%async_computation.4 | async-start | bytes 2228224 | tf_op jit(solution)/shard_map/reduce_scatter | solution.py:121
Sparse Core Ops, SparseCore 0:
  9.8 50.0 all-gather.2
  61.7 39.6 all-gather.4
  200.5 70.3 reduce-scatter.4
  274.3 79.2 reduce-scatter.2
where the time goes:
time: 362 us
  waiting for transfers between devices  233 us (64%)
  blocking collectives  89.8 us (25%)
  between operations  13.3 us (4%)
  local copies, waits for them, and re-layouts  12.5 us (3%)
  other arithmetic  6.67 us (2%)
  matrix products  6.66 us (2%)
    reduce_scatter x1, waiting for transfers between devices, body(): lax.psum_scatter(jnp.dot(part, candidates, preferred_element_type=jnp.flo...  82.7 us
    reduce_scatter x1, waiting for transfers between devices, body(): lax.psum_scatter(lax.dot_general(part, anchors, (((0,), (0,)), ((), ())),...  68.4 us
    psum x1, blocking collectives, body(): count_sum, slope_sum = lax.psum((count_part, slope_part), 'col')  56.1 us
    all_gather x1, waiting for transfers between devices, body(): candidates = lax.all_gather(embed, 'row', axis=0, tiled=True)  41.6 us
    all_gather x1, waiting for transfers between devices, body(): anchors = lax.all_gather(embed, 'col', axis=0, tiled=True)  38.6 us
    psum x1, blocking collectives, body(): matching_pair_affinity_lines = lax.psum(pos_part, 'col')  33.7 us
    gather x3, local copies, waits for them, and re-layouts, body(): targets = jnp.take(placement, positives)  12.1 us
  transfers between devices with their start and end apart: 4, of which 4 were waited for; matrix products, arithmetic and copies ran while one was open for 4% of the time, Pallas kernels for 0%

commit v1 on v0

v1 whole, which is shorter than its diff:
```python
import functools

import jax
import jax.numpy as jnp
from jax import lax
from jax.experimental import pallas as pl
from jax.experimental.pallas import tpu as pltpu
from jax.sharding import PartitionSpec as P

MESH = pl.DeviceIdType.MESH
TAU = 0.02
HALF = 0.5 / TAU
F32, BF16, I32 = jnp.float32, jnp.bfloat16, jnp.int32

ROWS, COLS, ZS = 16, 16, 8
SHARD, WIDTH, POS = 32, 1024, 4
BLOCK = SHARD * COLS
LANES = 128
STEP = 64

PLANE = (
    (2, 2), (2, 3), (3, 2), (2, 1), (1, 2), (2, 0), (0, 2), (3, 1),
    (1, 3), (3, 3), (1, 1), (3, 0), (0, 3), (1, 0), (0, 1),
)


def remote(src, dst, send, recv, device):
    return pltpu.make_async_remote_copy(
        src_ref=src, dst_ref=dst, send_sem=send, recv_sem=recv,
        device_id=device, device_id_type=MESH,
    )


def kernel(
    embed, positives, placement, out,
    a_buf, c_buf, s_ref, vi, vj, gi, gj, part, landed, mine,
    pos_in, place_in, tgt, pt, we, x1s, x1r, x2s, x2r, jp, jw, jt, jc,
    in_sem, plane_s, plane_r, z_s, z_r, sib_s, sib_r,
    x1_ss, x1_rs, x2_ss, x2_rs, p_ss, p_rs, w_ss, w_rs, g_ss, g_rs,
):
    r, c = lax.axis_index("row"), lax.axis_index("col")
    z, core = r // 2, r % 2
    y, x = c // 4, c % 4

    def in_plane(o):
        return (r, ((y + o[0]) % 4) * 4 + (x + o[1]) % 4)

    def in_line(d, k=0):
        return (((z + d) % ZS) * 2 + (core + k) % 2, c)

    loads = [
        pltpu.make_async_copy(embed, a_buf.at[c], in_sem.at[0]),
        pltpu.make_async_copy(embed, c_buf.at[r], in_sem.at[1]),
        pltpu.make_async_copy(positives, pos_in, in_sem.at[2]),
        pltpu.make_async_copy(placement, place_in, in_sem.at[3]),
    ]
    for load in loads:
        load.start()
    barrier = pltpu.get_barrier_semaphore()

    def greet(o, carry):
        pl.semaphore_signal(barrier, inc=1, device_id=(r, c ^ o), device_id_type=MESH)
        pl.semaphore_signal(barrier, inc=1, device_id=(r ^ o, c), device_id_type=MESH)
        return carry

    lax.fori_loop(1, 16, greet, 0)
    for load in loads:
        load.wait()
    pl.semaphore_wait(barrier, 30)

    sent, plane = [], []
    todo = iter(list(enumerate(PLANE)))

    def send_plane(count):
        for _ in range(count):
            i, o = next(todo)
            copy = remote(a_buf.at[c], a_buf.at[c], plane_s.at[i], plane_r.at[i], in_plane(o))
            copy.start()
            sent.append(copy)

    for i, d in enumerate((4, 3, 5, 2, 6, 1, 7)):
        copy = remote(c_buf.at[r], c_buf.at[r], z_s.at[d], z_r.at[d], in_line(d))
        copy.start()
        sent.append(copy)
        send_plane(2)
    own = remote(c_buf.at[r], c_buf.at[r], sib_s.at[0], sib_r.at[0], in_line(0, 1))
    own.start()
    sent.append(own)
    send_plane(1)

    table = place_in[...]
    high = (table // 64).astype(F32).astype(BF16)
    low = (table % 64).astype(F32).astype(BF16)
    lane_id = lax.broadcasted_iota(I32, (LANES, BLOCK), 0)
    row_id = lax.broadcasted_iota(I32, (64, BLOCK), 0)
    for m in range(POS):
        entity = pos_in[m : m + 1, :]
        hot = jnp.where(lane_id == entity % LANES, 1.0, 0.0).astype(BF16)
        value = jnp.dot(high, hot, preferred_element_type=F32) * 64.0 + jnp.dot(
            low, hot, preferred_element_type=F32
        )
        found = jnp.sum(jnp.where(row_id == entity // LANES, value, 0.0), axis=0, keepdims=True)
        pt[POS + m : POS + m + 1, :] = found
        where = found.astype(I32)
        here = (where // SHARD) % COLS == c
        tgt[m : m + 1, :] = jnp.where(here, (where // BLOCK) * SHARD + where % SHARD, -1)

    for d in (1, 7, 2, 6, 3, 5, 4):
        back = (((z + ZS - d) % ZS) * 2 + core) % ROWS
        remote(c_buf.at[back], c_buf.at[back], z_s.at[d], z_r.at[d], in_line(d)).wait_recv()
        copy = remote(c_buf.at[back], c_buf.at[back], sib_s.at[d], sib_r.at[d], in_line(0, 1))
        copy.start()
        sent.append(copy)
    for i, o in enumerate(PLANE):
        back = ((y + 4 - o[0]) % 4) * 4 + (x + 4 - o[1]) % 4
        remote(a_buf.at[back], a_buf.at[back], plane_s.at[i], plane_r.at[i], in_plane(o)).wait_recv()
    for d in range(ZS):
        back = ((z + ZS - d) % ZS) * 2 + (1 - core)
        remote(c_buf.at[back], c_buf.at[back], sib_s.at[d], sib_r.at[d], in_line(0, 1)).wait_recv()

    anchors = a_buf[...].reshape(BLOCK, WIDTH)
    for h in range(2):
        cand = c_buf[8 * h : 8 * h + 8].reshape(BLOCK // 2, WIDTH)
        s_ref[256 * h : 256 * h + 256, :] = HALF * lax.dot_general(
            cand, anchors, (((1,), (1,)), ((), ())), preferred_element_type=F32
        )
    tile = s_ref[pl.ds(pl.multiple_of(r * SHARD, SHARD), SHARD), pl.ds(pl.multiple_of(y * LANES, LANES), LANES)]
    me_row = lax.broadcasted_iota(I32, (SHARD, LANES), 0)
    me_lane = lax.broadcasted_iota(I32, (SHARD, LANES), 1)
    s_ref[pl.ds(pl.multiple_of(r * SHARD, SHARD), SHARD), pl.ds(pl.multiple_of(y * LANES, LANES), LANES)] = (
        jnp.where(me_lane - x * SHARD == me_row, -1e30, tile)
    )

    iota_k = lax.broadcasted_iota(I32, (STEP, LANES), 0)
    iota_a = lax.broadcasted_iota(I32, (STEP, LANES), 1)
    steps = BLOCK // STEP

    def fold(value):
        return jnp.sum(value.reshape(STEP // 8, 8, LANES), axis=0)

    def cut(q):
        return slice(q * LANES, (q + 1) * LANES)

    for q in range(4):
        rows = [tgt[m : m + 1, cut(q)] for m in range(POS)]

        def pick(i, acc, q=q, rows=rows):
            k0 = pl.multiple_of(i * STEP, STEP)
            score = s_ref[pl.ds(k0, STEP), cut(q)]
            return tuple(
                acc[m] + fold(jnp.where(iota_k == rows[m] - k0, score, 0.0)) for m in range(POS)
            )

        acc = lax.fori_loop(0, steps, pick, (jnp.zeros((8, LANES), F32),) * POS)
        for m in range(POS):
            half, lane = q // 2, (q % 2) * LANES
            x1s[half * POS + m : half * POS + m + 1, lane : lane + LANES] = jnp.sum(
                acc[m], axis=0, keepdims=True
            )

    def exchange(src, dst, ss, rs, peer):
        def start(o, carry):
            remote(src, dst, ss.at[o], rs.at[o], peer(o)).start()
            return carry

        lax.fori_loop(1, 16, start, 0)

    def arrive(src, dst, ss, rs, peer, index):
        def wait(o, carry):
            remote(src, dst.at[index ^ o], ss.at[o], rs.at[o], peer(o)).wait_recv()
            return carry

        lax.fori_loop(1, 16, wait, 0)

    def leave(src, dst, ss, rs, peer):
        def wait(o, carry):
            remote(src, dst, ss.at[o], rs.at[o], peer(o)).wait_send()
            return carry

        lax.fori_loop(1, 16, wait, 0)

    def peer_c(o):
        return (r, c ^ o)

    def peer_r(o):
        return (r ^ o, c)

    exchange(x1s, x1r.at[c], x1_ss, x1_rs, peer_c)
    x1r[c] = x1s[...]
    arrive(x1s, x1r, x1_ss, x1_rs, peer_c, c)
    total = jnp.sum(x1r[...], axis=0)
    pt[0:POS, 0:256] = total[0:POS]
    pt[0:POS, 256:512] = total[POS : 2 * POS]

    group = pl.ds(pl.multiple_of(y * LANES, LANES), LANES)
    exchange(pt.at[:, group], jp.at[r], p_ss, p_rs, peer_r)
    jp[r] = pt[:, group]

    for q in range(4):
        rows = [pt[m : m + 1, cut(q)] for m in range(POS)]

        def count(i, acc, q=q, rows=rows):
            k0 = pl.multiple_of(i * STEP, STEP)
            score = s_ref[pl.ds(k0, STEP), cut(q)]
            new = []
            for m in range(POS):
                u = 1.0 + jnp.tanh(score - rows[m])
                v = u * (2.0 - u)
                vi[m, pl.ds(k0, STEP), cut(q)] = v
                new.append(acc[2 * m] + fold(u))
                new.append(acc[2 * m + 1] + fold(v))
            return tuple(new)

        acc = lax.fori_loop(0, steps, count, (jnp.zeros((8, LANES), F32),) * (2 * POS))
        for m in range(POS):
            x2s[m : m + 1, cut(q)] = jnp.sum(acc[2 * m], axis=0, keepdims=True)
            x2s[POS + m : POS + m + 1, cut(q)] = jnp.sum(acc[2 * m + 1], axis=0, keepdims=True)
    exchange(x2s, x2r.at[c], x2_ss, x2_rs, peer_c)
    x2r[c] = x2s[...]

    def columns(src, first):
        jt[...] = jnp.transpose(src[...].reshape(ROWS * 8, LANES))
        mine_cols = jt[pl.ds(pl.multiple_of(x * SHARD, SHARD), SHARD), :]
        for b in range(ROWS):
            for n in range(8):
                jc[first + n, b * SHARD : (b + 1) * SHARD, :] = jnp.broadcast_to(
                    mine_cols[:, b * 8 + n : b * 8 + n + 1], (SHARD, LANES)
                )

    arrive(pt.at[:, group], jp, p_ss, p_rs, peer_r, r)
    columns(jp, 0)

    def slopes(i, carry):
        k0 = pl.multiple_of(i * STEP, STEP)
        for m in range(POS):
            col = jc[m, pl.ds(k0, STEP), :]
            for q in range(4):
                u = 1.0 + jnp.tanh(s_ref[pl.ds(k0, STEP), cut(q)] - col)
                vj[m, pl.ds(k0, STEP), cut(q)] = u * (2.0 - u)
            where = jc[POS + m, pl.ds(k0, STEP), :].astype(I32)
            jc[POS + m, pl.ds(k0, STEP), :] = jnp.where(
                where // BLOCK == r, where % BLOCK, -1
            ).astype(F32)
        return carry

    lax.fori_loop(0, steps, slopes, 0)

    arrive(x2s, x2r, x2_ss, x2_rs, peer_c, c)
    total = jnp.sum(x2r[...], axis=0)
    factor = 1.0 / (POS * SHARD * ROWS * COLS)
    p = [pt[m : m + 1, :] for m in range(POS)]
    rank = [0.5 + 0.5 * total[m : m + 1] for m in range(POS)]
    slope = [0.25 * total[POS + m : POS + m + 1] for m in range(POS)]
    prank = [jnp.full((1, BLOCK), 1.0, F32) for _ in range(POS)]
    grad = [-factor / rank[m] for m in range(POS)]
    pulled = [jnp.zeros((1, BLOCK), F32) for _ in range(POS)]
    for m in range(POS):
        for n in range(m + 1, POS):
            t = jnp.tanh(p[n] - p[m])
            prank[m] = prank[m] + 0.5 * (1.0 + t)
            prank[n] = prank[n] + 0.5 * (1.0 - t)
            pair = (0.25 / TAU) * (1.0 - t) * (1.0 + t) * (grad[n] - grad[m])
            pulled[m] = pulled[m] + pair
            pulled[n] = pulled[n] - pair
    for m in range(POS):
        weight = prank[m] / (rank[m] * rank[m]) * factor / TAU
        we[m : m + 1, :] = 0.25 * weight
        we[POS + m : POS + m + 1, :] = pulled[m] - weight * slope[m]

    exchange(we.at[:, group], jw.at[r], w_ss, w_rs, peer_r)
    jw[r] = we[:, group]

    for q in range(4):
        rows = [tgt[m : m + 1, cut(q)] for m in range(POS)]
        weights = [we[m : m + 1, cut(q)] for m in range(POS)]
        extras = [we[POS + m : POS + m + 1, cut(q)] for m in range(POS)]

        def tile_i(i, carry, q=q, rows=rows, weights=weights, extras=extras):
            k0 = pl.multiple_of(i * STEP, STEP)
            dense = weights[0] * vi[0, pl.ds(k0, STEP), cut(q)]
            for m in range(1, POS):
                dense = dense + weights[m] * vi[m, pl.ds(k0, STEP), cut(q)]
            for m in range(POS):
                dense = dense + jnp.where(iota_k == rows[m] - k0, extras[m], 0.0)
            gi[pl.ds(k0, STEP), cut(q)] = dense.astype(BF16)
            return carry

        lax.fori_loop(0, steps, tile_i, 0)

    arrive(we.at[:, group], jw, w_ss, w_rs, peer_r, r)
    columns(jw, 2 * POS)

    cand = c_buf[...].reshape(BLOCK, WIDTH)
    wide = 2 * LANES
    for h in range(2):
        def tile_j(i, carry, h=h):
            k0 = pl.multiple_of(i * STEP, STEP)
            for q in (2 * h, 2 * h + 1):
                dense = jc[2 * POS, pl.ds(k0, STEP), :] * vj[0, pl.ds(k0, STEP), cut(q)]
                for m in range(1, POS):
                    dense = dense + jc[2 * POS + m, pl.ds(k0, STEP), :] * vj[m, pl.ds(k0, STEP), cut(q)]
                lane = (iota_a + q * LANES).astype(F32)
                for m in range(POS):
                    dense = dense + jnp.where(
                        jc[POS + m, pl.ds(k0, STEP), :] == lane,
                        jc[3 * POS + m, pl.ds(k0, STEP), :],
                        0.0,
                    )
                gj[pl.ds(k0, STEP), cut(q)] = dense.astype(BF16)
            return carry

        lax.fori_loop(0, steps, tile_j, 0)
        half = slice(h * wide, (h + 1) * wide)
        dims = (((0,), (0,)), ((), ()))
        product = lax.dot_general(gi[:, half], cand, dims, preferred_element_type=F32)
        product = product + lax.dot_general(gj[:, half], cand, dims, preferred_element_type=F32)
        part[8 * h : 8 * h + 8] = product.astype(BF16).reshape(8, SHARD, WIDTH)

        @pl.when(c // 8 == h)
        def _(product=product, h=h):
            mine[...] = product.reshape(8, SHARD, WIDTH)

        def push(n, carry, h=h):
            to = 8 * h + n

            @pl.when(to != c)
            def _():
                remote(part.at[to], landed.at[c], g_ss.at[to], g_rs.at[c], (r, to)).start()

            return carry

        lax.fori_loop(0, 8, push, 0)

    out[...] = mine[c % 8]

    def gather_sum(o, carry):
        frm = c ^ o
        remote(part.at[frm], landed.at[frm], g_ss.at[frm], g_rs.at[frm], (r, frm)).wait_recv()
        out[...] += landed[frm].astype(F32)
        return carry

    lax.fori_loop(1, 16, gather_sum, 0)

    def sent_all(o, carry):
        frm = c ^ o
        remote(part.at[frm], landed.at[frm], g_ss.at[frm], g_rs.at[frm], (r, frm)).wait_send()
        return carry

    lax.fori_loop(1, 16, sent_all, 0)
    leave(x1s, x1r.at[c], x1_ss, x1_rs, peer_c)
    leave(x2s, x2r.at[c], x2_ss, x2_rs, peer_c)
    leave(pt.at[:, group], jp.at[r], p_ss, p_rs, peer_r)
    leave(we.at[:, group], jw.at[r], w_ss, w_rs, peer_r)
    for copy in sent:
        copy.wait_send()


def body(embed, positives, placement):
    dma = pltpu.SemaphoreType.DMA
    return pl.pallas_call(
        kernel,
        out_shape=jax.ShapeDtypeStruct((SHARD, WIDTH), F32),
        in_specs=[pl.BlockSpec(memory_space=pl.ANY)] * 3,
        out_specs=pl.BlockSpec(memory_space=pltpu.VMEM),
        scratch_shapes=[
            pltpu.VMEM((COLS, SHARD, WIDTH), BF16),
            pltpu.VMEM((ROWS, SHARD, WIDTH), BF16),
            pltpu.VMEM((BLOCK, BLOCK), F32),
            pltpu.VMEM((POS, BLOCK, BLOCK), F32),
            pltpu.VMEM((POS, BLOCK, BLOCK), F32),
            pltpu.VMEM((BLOCK, BLOCK), BF16),
            pltpu.VMEM((BLOCK, BLOCK), BF16),
            pltpu.VMEM((COLS, SHARD, WIDTH), BF16),
            pltpu.VMEM((COLS, SHARD, WIDTH), BF16),
            pltpu.VMEM((8, SHARD, WIDTH), F32),
            pltpu.VMEM((POS, BLOCK), I32),
            pltpu.VMEM((64, LANES), I32),
            pltpu.VMEM((8, BLOCK), I32),
            pltpu.VMEM((8, BLOCK), F32),
            pltpu.VMEM((8, BLOCK), F32),
            pltpu.VMEM((8, BLOCK // 2), F32),
            pltpu.VMEM((COLS, 8, BLOCK // 2), F32),
            pltpu.VMEM((8, BLOCK), F32),
            pltpu.VMEM((COLS, 8, BLOCK), F32),
            pltpu.VMEM((ROWS, 8, LANES), F32),
            pltpu.VMEM((ROWS, 8, LANES), F32),
            pltpu.VMEM((LANES, LANES), F32),
            pltpu.VMEM((4 * POS, BLOCK, LANES), F32),
            dma((4,)),
        ]
        + [dma((16,))] * 16,
        compiler_params=pltpu.CompilerParams(
            collective_id=0, has_side_effects=True, vmem_limit_bytes=48 * 1024 * 1024
        ),
        cost_estimate=pl.CostEstimate(flops=1 << 31, bytes_accessed=1 << 22, transcendentals=1 << 21),
        name="smooth_ap",
    )(embed, positives.T, placement.reshape(64, LANES))


def solution(mesh):
    return jax.shard_map(
        body,
        mesh=mesh,
        in_specs=(P(("row", "col"), None), P("row", None), P()),
        out_specs=P(("row", "col"), None),
        check_vma=False,
    )
```

time: 362 us -> 70.5 us (0.19)
  waiting for transfers between devices: 233 us -> 0 us
  blocking collectives: 89.8 us -> 0 us
  Pallas kernels: 0 us -> 66.8 us
  between operations: 13.3 us -> 0.01 us
  local copies, waits for them, and re-layouts: 12.5 us -> 2.95 us
  other arithmetic: 6.67 us -> 0 us
  matrix products: 6.66 us -> 0 us
    reduce_scatter x2 -> x0, waiting for transfers between devices: 151 us -> none  [the longest x1 82.7 us: body(): lax.psum_scatter(jnp.dot(part, candidates, preferred_element_type=jnp.flo...]
    psum x2 -> x0, blocking collectives: 89.8 us -> none  [the longest x1 56.1 us: body(): count_sum, slope_sum = lax.psum((count_part, slope_part), 'col')]
    all_gather x2 -> x0, waiting for transfers between devices: 80.2 us -> none  [the longest x1 41.6 us: body(): candidates = lax.all_gather(embed, 'row', axis=0, tiled=True)]
    pallas_call x0 -> x1, Pallas kernels: none -> 66.8 us  [body(): pl.pallas_call(kernel, out_shape=jax.ShapeDtypeStruct((SHARD, WIDTH), F32...]
    gather x3 -> x0, local copies, waits for them, and re-layouts: 12.1 us -> none  [body(): targets = jnp.take(placement, positives)]
    dot_general x3 -> x0, matrix products: 6.66 us -> none  [the longest x1 2.57 us: body(): jnp.einsum('ad,kd->ak', anchors, candidates, preferred_element_type=jnp.f...]
  transfers between devices with their start and end apart: 4 -> 0, of which waited for: 4 -> 0; matrix products, arithmetic and copies ran while one was open for 4% -> 0% of each run, Pallas kernels for 0% -> 0%
where the time goes in v1:
time: 70.5 us; the launch traced here: 69.8 us
  Pallas kernels  66.8 us (95%)
  local copies, waits for them, and re-layouts  2.95 us (4%)
    pallas_call x1, Pallas kernels, body(): pl.pallas_call(kernel, out_shape=jax.ShapeDtypeStruct((SHARD, WIDTH), F32...  66.8 us
    unnamed x7, local copies, waits for them, and re-layouts  2.95 us

profile of v1, /device:TPU:1, one launch (start us, length us, event | category | flops | bytes accessed | tf_op | source)
XLA Modules:
  0.0 69.8 jit_solution(2502169696829719502)
XLA Ops:
  0.0 0.0 copy-start
  0.0 0.8 %copy-done = bf16[32,1024]{1,0:T(8,128)(2,1)S(1)} copy-done((bf16[32,1024]{1,0:T(8,128)(2,1)S(1)}, bf16[32,1024]{1,0:T(8,128)(2,1)}, u32[]{:S(2)}) %copy-start) | copy-done | bytes 65560
  0.8 0.0 copy-start.1
  0.8 0.8 %copy-done.1 = s32[8192]{0:T(1024)S(1)} copy-done((s32[8192]{0:T(1024)S(1)}, s32[8192]{0:T(1024)}, u32[]{:S(2)}) %copy-start.1) | copy-done | bytes 32792
  1.6 0.0 copy-start.2
  1.6 0.7 copy-done.2
  2.3 66.8 %smooth_ap.1 = f32[32,1024]{1,0:T(8,128)S(1)} custom-call(bf16[32,1024]{1,0:T(8,128)(2,1)S(1)} %copy-done, s32[4,512]{1,0:T(4,128)S(1)} %bitcast.3, s32[64,128]{1,0:T(8,128)S(1)} %bitcast.2), custom_call_target="tpu_custom_call" | custom-call | flops 2147483648 | bytes 4194304 | tf_op jit(solution)/shard_map/smooth_ap/pallas_call | solution.py:360
  69.1 0.7 copy.5
Async XLA Ops:
  0.0 0.8 %copy-start = (bf16[32,1024]{1,0:T(8,128)(2,1)S(1)}, bf16[32,1024]{1,0:T(8,128)(2,1)}, u32[]{:S(2)}) copy-start(bf16[32,1024]{1,0:T(8,128)(2,1)} %embed.1) | copy-start | bytes 196612
  0.8 0.8 %copy-start.1 = (s32[8192]{0:T(1024)S(1)}, s32[8192]{0:T(1024)}, u32[]{:S(2)}) copy-start(s32[8192]{0:T(1024)} %param.5) | copy-start | bytes 98308
  1.6 0.7 copy-start.2

commit v2 on v1

--- a/solution.py
+++ b/solution.py
@@ -18,9 +18,12 @@
 LANES = 128
 STEP = 64
 
-PLANE = (
-    (2, 2), (2, 3), (3, 2), (2, 1), (1, 2), (2, 0), (0, 2), (3, 1),
-    (1, 3), (3, 3), (1, 1), (3, 0), (0, 3), (1, 0), (0, 1),
+NARROW = 256
+BROAD = WIDTH - NARROW
+
+LINE = (
+    (4, 0), (3, 1), (5, 0), (4, 1), (3, 0), (5, 1), (2, 0), (6, 1),
+    (2, 1), (6, 0), (1, 0), (7, 1), (1, 1), (7, 0), (0, 1),
 )
 
 
@@ -33,10 +36,10 @@
 
 def kernel(
     embed, positives, placement, out,
-    a_buf, c_buf, s_ref, vi, vj, gi, gj, part, landed, mine,
+    a_buf, c_buf, s_ref, vi, vj, gi, gj, part, landed, mine, z_part, z_landed, z_mine,
     pos_in, place_in, tgt, pt, we, x1s, x1r, x2s, x2r, jp, jw, jt, jc,
     in_sem, plane_s, plane_r, z_s, z_r, sib_s, sib_r,
-    x1_ss, x1_rs, x2_ss, x2_rs, p_ss, p_rs, w_ss, w_rs, g_ss, g_rs,
+    x1_ss, x1_rs, x2_ss, x2_rs, p_ss, p_rs, w_ss, w_rs, g_ss, g_rs, h_ss, h_rs,
 ):
     r, c = lax.axis_index("row"), lax.axis_index("col")
     z, core = r // 2, r % 2
@@ -68,25 +71,54 @@
         load.wait()
     pl.semaphore_wait(barrier, 30)
 
-    sent, plane = [], []
-    todo = iter(list(enumerate(PLANE)))
-
-    def send_plane(count):
-        for _ in range(count):
-            i, o = next(todo)
-            copy = remote(a_buf.at[c], a_buf.at[c], plane_s.at[i], plane_r.at[i], in_plane(o))
-            copy.start()
-            sent.append(copy)
-
-    for i, d in enumerate((4, 3, 5, 2, 6, 1, 7)):
-        copy = remote(c_buf.at[r], c_buf.at[r], z_s.at[d], z_r.at[d], in_line(d))
+    sent = []
+
+    def go(src, dst, ss, rs, device):
+        copy = remote(src, dst, ss, rs, device)
         copy.start()
         sent.append(copy)
-        send_plane(2)
-    own = remote(c_buf.at[r], c_buf.at[r], sib_s.at[0], sib_r.at[0], in_line(0, 1))
-    own.start()
-    sent.append(own)
-    send_plane(1)
+
+    def z_send(d, block, rows, step, slot):
+        view = c_buf.at[block, rows]
+        go(view, view, z_s.at[slot], z_r.at[slot], in_line(step % ZS))
+
+    def z_wait(d, rows, slot):
+        view = c_buf.at[from_z(d), rows]
+        remote(view, view, z_s.at[slot], z_r.at[slot], in_line(d % ZS)).wait_recv()
+
+    def from_z(d, k=0):
+        return ((z + ZS - d) % ZS) * 2 + (core + k) % 2
+
+    def from_plane(dy, dx):
+        return ((y + 4 - dy) % 4) * 4 + (x + 4 - dx) % 4
+
+    def a_send(block, rows, dy, dx, slot):
+        view = a_buf.at[block, rows]
+        go(view, view, plane_s.at[slot], plane_r.at[slot], in_plane((dy, dx)))
+
+    def a_wait(dy, dx, rows, slot):
+        view = a_buf.at[from_plane(dy, dx), rows]
+        remote(view, view, plane_s.at[slot], plane_r.at[slot], in_plane((dy, dx))).wait_recv()
+
+    def sib_send(d, rows, slot):
+        view = c_buf.at[from_z(d), rows]
+        go(view, view, sib_s.at[slot], sib_r.at[slot], in_line(0, 1))
+
+    def sib_wait(d, rows, slot):
+        view = c_buf.at[from_z(d, 1), rows]
+        remote(view, view, sib_s.at[slot], sib_r.at[slot], in_line(0, 1)).wait_recv()
+
+    every, top, low_half = pl.ds(0, SHARD), pl.ds(0, SHARD // 2), pl.ds(SHARD // 2, SHARD // 2)
+    z_send(2, r, every, 2, 2)
+    z_send(-2, r, every, -2, 6)
+    a_send(c, every, 0, 2, 1)
+    a_send(c, every, 2, 0, 4)
+    z_send(1, r, every, 1, 1)
+    z_send(-1, r, every, -1, 7)
+    for d in (1, 3):
+        a_send(c, every, 0, d, d - 1)
+        a_send(c, every, d, 0, d + 2)
+    sib_send(0, every, 0)
 
     table = place_in[...]
     high = (table // 64).astype(F32).astype(BF16)
@@ -105,18 +137,43 @@
         here = (where // SHARD) % COLS == c
         tgt[m : m + 1, :] = jnp.where(here, (where // BLOCK) * SHARD + where % SHARD, -1)
 
-    for d in (1, 7, 2, 6, 3, 5, 4):
-        back = (((z + ZS - d) % ZS) * 2 + core) % ROWS
-        remote(c_buf.at[back], c_buf.at[back], z_s.at[d], z_r.at[d], in_line(d)).wait_recv()
-        copy = remote(c_buf.at[back], c_buf.at[back], sib_s.at[d], sib_r.at[d], in_line(0, 1))
-        copy.start()
-        sent.append(copy)
-    for i, o in enumerate(PLANE):
-        back = ((y + 4 - o[0]) % 4) * 4 + (x + 4 - o[1]) % 4
-        remote(a_buf.at[back], a_buf.at[back], plane_s.at[i], plane_r.at[i], in_plane(o)).wait_recv()
-    for d in range(ZS):
-        back = ((z + ZS - d) % ZS) * 2 + (1 - core)
-        remote(c_buf.at[back], c_buf.at[back], sib_s.at[d], sib_r.at[d], in_line(0, 1)).wait_recv()
+    def turn(d):
+        a_wait(0, d, every, d - 1)
+        for e in (2, 1, 3):
+            a_send(from_plane(0, d), top, e, 0, 6 + 3 * (d - 1) + e - 1)
+        a_wait(d, 0, every, d + 2)
+        for e in (2, 1, 3):
+            a_send(from_plane(d, 0), low_half, 0, e, 15 + 3 * (d - 1) + e - 1)
+
+    turn(1)
+    turn(3)
+    z_wait(2, every, 2)
+    z_send(4, from_z(2), top, 2, 4)
+    z_send(3, from_z(2), every, 1, 3)
+    z_wait(-2, every, 6)
+    z_send(-4, from_z(-2), low_half, -2, 8)
+    z_send(-3, from_z(-2), every, -1, 5)
+    turn(2)
+    for d, slot in ((2, 2), (-2, 6)):
+        sib_send(d, every, slot)
+    for d, slot in ((1, 1), (-1, 7)):
+        z_wait(d, every, slot)
+        sib_send(d, every, slot)
+    for d, slot in ((3, 3), (-3, 5)):
+        z_wait(d, every, slot)
+        sib_send(d, every, slot)
+    z_wait(4, top, 4)
+    sib_send(4, top, 4)
+    z_wait(-4, low_half, 8)
+    sib_send(-4, low_half, 8)
+    for d in (1, 3, 2):
+        for e in (1, 3, 2):
+            a_wait(e, d, top, 6 + 3 * (d - 1) + e - 1)
+            a_wait(d, e, low_half, 15 + 3 * (d - 1) + e - 1)
+    for d, slot in ((0, 0), (1, 1), (-1, 7), (2, 2), (-2, 6), (3, 3), (-3, 5)):
+        sib_wait(d, every, slot)
+    sib_wait(4, top, 4)
+    sib_wait(-4, low_half, 8)
 
     anchors = a_buf[...].reshape(BLOCK, WIDTH)
     for h in range(2):
@@ -229,21 +286,6 @@
 
     arrive(pt.at[:, group], jp, p_ss, p_rs, peer_r, r)
     columns(jp, 0)
-
-    def slopes(i, carry):
-        k0 = pl.multiple_of(i * STEP, STEP)
-        for m in range(POS):
-            col = jc[m, pl.ds(k0, STEP), :]
-            for q in range(4):
-                u = 1.0 + jnp.tanh(s_ref[pl.ds(k0, STEP), cut(q)] - col)
-                vj[m, pl.ds(k0, STEP), cut(q)] = u * (2.0 - u)
-            where = jc[POS + m, pl.ds(k0, STEP), :].astype(I32)
-            jc[POS + m, pl.ds(k0, STEP), :] = jnp.where(
-                where // BLOCK == r, where % BLOCK, -1
-            ).astype(F32)
-        return carry
-
-    lax.fori_loop(0, steps, slopes, 0)
 
     arrive(x2s, x2r, x2_ss, x2_rs, peer_c, c)
     total = jnp.sum(x2r[...], axis=0)
@@ -287,66 +329,100 @@
 
         lax.fori_loop(0, steps, tile_i, 0)
 
+    def slopes(i, carry):
+        k0 = pl.multiple_of(i * STEP, STEP)
+        for m in range(POS):
+            col = jc[m, pl.ds(k0, STEP), :]
+            for q in range(4):
+                u = 1.0 + jnp.tanh(s_ref[pl.ds(k0, STEP), cut(q)] - col)
+                vj[m, pl.ds(k0, STEP), cut(q)] = u * (2.0 - u)
+            where = jc[POS + m, pl.ds(k0, STEP), :].astype(I32)
+            jc[POS + m, pl.ds(k0, STEP), :] = jnp.where(
+                where // BLOCK == r, where % BLOCK, -1
+            ).astype(F32)
+        return carry
+
+    lax.fori_loop(0, steps, slopes, 0)
+
     arrive(we.at[:, group], jw, w_ss, w_rs, peer_r, r)
     columns(jw, 2 * POS)
 
-    cand = c_buf[...].reshape(BLOCK, WIDTH)
+    def tile_j(i, carry):
+        k0 = pl.multiple_of(i * STEP, STEP)
+        for q in range(4):
+            dense = jc[2 * POS, pl.ds(k0, STEP), :] * vj[0, pl.ds(k0, STEP), cut(q)]
+            for m in range(1, POS):
+                dense = dense + jc[2 * POS + m, pl.ds(k0, STEP), :] * vj[m, pl.ds(k0, STEP), cut(q)]
+            lane = (iota_a + q * LANES).astype(F32)
+            for m in range(POS):
+                dense = dense + jnp.where(
+                    jc[POS + m, pl.ds(k0, STEP), :] == lane,
+                    jc[3 * POS + m, pl.ds(k0, STEP), :],
+                    0.0,
+                )
+            gj[pl.ds(k0, STEP), cut(q)] = dense.astype(BF16)
+        return carry
+
+    lax.fori_loop(0, steps, tile_j, 0)
+
+    right = a_buf[:, :, BROAD:].reshape(BLOCK, NARROW)
+    for h in range(2):
+        rows = slice(256 * h, 256 * h + 256)
+        product = jnp.dot(gi[rows, :], right, preferred_element_type=F32)
+        product = product + jnp.dot(gj[rows, :], right, preferred_element_type=F32)
+        z_part[8 * h : 8 * h + 8] = product.astype(BF16).reshape(8, SHARD, NARROW)
+
+        @pl.when(r // 8 == h)
+        def _(product=product):
+            z_mine[...] = product.reshape(8, SHARD, NARROW)
+
+    for i, o in enumerate(LINE):
+        to = ((z + o[0]) % ZS) * 2 + (core + o[1]) % 2
+        remote(z_part.at[to], z_landed.at[r], h_ss.at[i], h_rs.at[i], (to, c)).start()
+
+    left = c_buf[:, :, :BROAD].reshape(BLOCK, BROAD)
     wide = 2 * LANES
-    for h in range(2):
-        def tile_j(i, carry, h=h):
-            k0 = pl.multiple_of(i * STEP, STEP)
-            for q in (2 * h, 2 * h + 1):
-                dense = jc[2 * POS, pl.ds(k0, STEP), :] * vj[0, pl.ds(k0, STEP), cut(q)]
-                for m in range(1, POS):
-                    dense = dense + jc[2 * POS + m, pl.ds(k0, STEP), :] * vj[m, pl.ds(k0, STEP), cut(q)]
-                lane = (iota_a + q * LANES).astype(F32)
-                for m in range(POS):
-                    dense = dense + jnp.where(
-                        jc[POS + m, pl.ds(k0, STEP), :] == lane,
-                        jc[3 * POS + m, pl.ds(k0, STEP), :],
-                        0.0,
-                    )
-                gj[pl.ds(k0, STEP), cut(q)] = dense.astype(BF16)
+    dims = (((0,), (0,)), ((), ()))
+    for turn_id in range(2):
+        h = (c // 8) ^ (1 - turn_id)
+        half = pl.ds(pl.multiple_of(h * wide, wide), wide)
+        product = lax.dot_general(gi[:, half], left, dims, preferred_element_type=F32)
+        product = product + lax.dot_general(gj[:, half], left, dims, preferred_element_type=F32)
+        part[pl.ds(h * 8, 8)] = product.astype(BF16).reshape(8, SHARD, BROAD)
+        if turn_id == 1:
+            mine[...] = product.reshape(8, SHARD, BROAD)
+
+        def push(n, carry):
+            to = c ^ n
+            remote(part.at[to], landed.at[c], g_ss.at[n], g_rs.at[n], (r, to)).start()
             return carry
 
-        lax.fori_loop(0, steps, tile_j, 0)
-        half = slice(h * wide, (h + 1) * wide)
-        dims = (((0,), (0,)), ((), ()))
-        product = lax.dot_general(gi[:, half], cand, dims, preferred_element_type=F32)
-        product = product + lax.dot_general(gj[:, half], cand, dims, preferred_element_type=F32)
-        part[8 * h : 8 * h + 8] = product.astype(BF16).reshape(8, SHARD, WIDTH)
-
-        @pl.when(c // 8 == h)
-        def _(product=product, h=h):
-            mine[...] = product.reshape(8, SHARD, WIDTH)
-
-        def push(n, carry, h=h):
-            to = 8 * h + n
-
-            @pl.when(to != c)
-            def _():
-                remote(part.at[to], landed.at[c], g_ss.at[to], g_rs.at[c], (r, to)).start()
-
-            return carry
-
-        lax.fori_loop(0, 8, push, 0)
-
-    out[...] = mine[c % 8]
+        lax.fori_loop(*((8, 16) if turn_id == 0 else (1, 8)), push, 0)
+
+    out[:, BROAD:] = z_mine[r % 8]
+    out[:, :BROAD] = mine[c % 8]
+    for i, o in reversed(list(enumerate(LINE))):
+        frm = from_z(o[0], o[1])
+        remote(z_part.at[frm], z_landed.at[frm], h_ss.at[i], h_rs.at[i], (frm, c)).wait_recv()
+        out[:, BROAD:] += z_landed[frm].astype(F32)
 
     def gather_sum(o, carry):
         frm = c ^ o
-        remote(part.at[frm], landed.at[frm], g_ss.at[frm], g_rs.at[frm], (r, frm)).wait_recv()
-        out[...] += landed[frm].astype(F32)
+        remote(part.at[frm], landed.at[frm], g_ss.at[o], g_rs.at[o], (r, frm)).wait_recv()
+        out[:, :BROAD] += landed[frm].astype(F32)
         return carry
 
     lax.fori_loop(1, 16, gather_sum, 0)
 
     def sent_all(o, carry):
         frm = c ^ o
-        remote(part.at[frm], landed.at[frm], g_ss.at[frm], g_rs.at[frm], (r, frm)).wait_send()
+        remote(part.at[frm], landed.at[frm], g_ss.at[o], g_rs.at[o], (r, frm)).wait_send()
         return carry
 
     lax.fori_loop(1, 16, sent_all, 0)
+    for i, o in enumerate(LINE):
+        to = ((z + o[0]) % ZS) * 2 + (core + o[1]) % 2
+        remote(z_part.at[to], z_landed.at[r], h_ss.at[i], h_rs.at[i], (to, c)).wait_send()
     leave(x1s, x1r.at[c], x1_ss, x1_rs, peer_c)
     leave(x2s, x2r.at[c], x2_ss, x2_rs, peer_c)
     leave(pt.at[:, group], jp.at[r], p_ss, p_rs, peer_r)
@@ -370,9 +446,12 @@
             pltpu.VMEM((POS, BLOCK, BLOCK), F32),
             pltpu.VMEM((BLOCK, BLOCK), BF16),
             pltpu.VMEM((BLOCK, BLOCK), BF16),
-            pltpu.VMEM((COLS, SHARD, WIDTH), BF16),
-            pltpu.VMEM((COLS, SHARD, WIDTH), BF16),
-            pltpu.VMEM((8, SHARD, WIDTH), F32),
+            pltpu.VMEM((COLS, SHARD, BROAD), BF16),
+            pltpu.VMEM((COLS, SHARD, BROAD), BF16),
+            pltpu.VMEM((8, SHARD, BROAD), F32),
+            pltpu.VMEM((ROWS, SHARD, NARROW), BF16),
+            pltpu.VMEM((ROWS, SHARD, NARROW), BF16),
+            pltpu.VMEM((8, SHARD, NARROW), F32),
             pltpu.VMEM((POS, BLOCK), I32),
             pltpu.VMEM((64, LANES), I32),
             pltpu.VMEM((8, BLOCK), I32),
@@ -387,10 +466,12 @@
             pltpu.VMEM((LANES, LANES), F32),
             pltpu.VMEM((4 * POS, BLOCK, LANES), F32),
             dma((4,)),
+            dma((24,)),
+            dma((24,)),
         ]
         + [dma((16,))] * 16,
         compiler_params=pltpu.CompilerParams(
-            collective_id=0, has_side_effects=True, vmem_limit_bytes=48 * 1024 * 1024
+            collective_id=0, has_side_effects=True, vmem_limit_bytes=60 * 1024 * 1024
         ),
         cost_estimate=pl.CostEstimate(flops=1 << 31, bytes_accessed=1 << 22, transcendentals=1 << 21),
         name="smooth_ap",

time: 70.5 us -> 62.3 us (0.88)
  Pallas kernels: 66.8 us -> 60.6 us
  local copies, waits for them, and re-layouts: 2.95 us -> 1.57 us
    pallas_call x1, Pallas kernels: 66.8 us -> 60.6 us  [body(): pl.pallas_call(kernel, out_shape=jax.ShapeDtypeStruct((SHARD, WIDTH), F32...]
    unnamed x7 -> x1, local copies, waits for them, and re-layouts: 2.95 us -> 1.57 us
where the time goes in v2:
time: 62.3 us; the launch traced here: 62.2 us
  Pallas kernels  60.6 us (97%)
  local copies, waits for them, and re-layouts  1.57 us (3%)
    pallas_call x1, Pallas kernels, body(): pl.pallas_call(kernel, out_shape=jax.ShapeDtypeStruct((SHARD, WIDTH), F32...  60.6 us
    unnamed x1, local copies, waits for them, and re-layouts  1.57 us

profile of v2, /device:TPU:1, one launch (start us, length us, event | category | flops | bytes accessed | tf_op | source)
XLA Modules:
  0.0 62.2 jit_solution(15671741473893721689)
XLA Ops:
  0.0 60.6 %smooth_ap.1 = f32[32,1024]{1,0:T(8,128)} custom-call(bf16[32,1024]{1,0:T(8,128)(2,1)} %embed.1, s32[4,512]{1,0:T(4,128)} %bitcast.3, s32[64,128]{1,0:T(8,128)} %bitcast.2), custom_call_target="tpu_custom_call" | custom-call | flops 2147483648 | bytes 4194304 | tf_op jit(solution)/shard_map/smooth_ap/pallas_call | solution.py:436
  60.6 1.6 %copy.5 = f32[32,1024]{1,0:T(8,128)} copy(f32[32,1024]{1,0:T(8,128)} %smooth_ap.1) | data formatting | bytes 262144

commit v3 on v2

--- a/solution.py
+++ b/solution.py
@@ -18,8 +18,8 @@
 LANES = 128
 STEP = 64
 
-NARROW = 256
-BROAD = WIDTH - NARROW
+BROAD, NARROW = 512, 256
+LINE_AT, BOTH_AT = BROAD, BROAD + NARROW
 
 LINE = (
     (4, 0), (3, 1), (5, 0), (4, 1), (3, 0), (5, 1), (2, 0), (6, 1),
@@ -37,9 +37,11 @@
 def kernel(
     embed, positives, placement, out,
     a_buf, c_buf, s_ref, vi, vj, gi, gj, part, landed, mine, z_part, z_landed, z_mine,
+    ez_part, ez_landed, ep_part, ep_landed,
     pos_in, place_in, tgt, pt, we, x1s, x1r, x2s, x2r, jp, jw, jt, jc,
     in_sem, plane_s, plane_r, z_s, z_r, sib_s, sib_r,
     x1_ss, x1_rs, x2_ss, x2_rs, p_ss, p_rs, w_ss, w_rs, g_ss, g_rs, h_ss, h_rs,
+    e_ss, e_rs, f_ss, f_rs,
 ):
     r, c = lax.axis_index("row"), lax.axis_index("col")
     z, core = r // 2, r % 2
@@ -250,8 +252,24 @@
     pt[0:POS, 256:512] = total[POS : 2 * POS]
 
     group = pl.ds(pl.multiple_of(y * LANES, LANES), LANES)
-    exchange(pt.at[:, group], jp.at[r], p_ss, p_rs, peer_r)
-    jp[r] = pt[:, group]
+    def line_copy(i, part_ref, landed_ref, ss, rs):
+        o = LINE[i]
+        to = ((z + o[0]) % ZS) * 2 + (core + o[1]) % 2
+        return remote(part_ref.at[to], landed_ref.at[r], ss.at[i], rs.at[i], (to, c))
+
+    def line_start(part_ref, landed_ref, ss, rs):
+        for i in range(15):
+            line_copy(i, part_ref, landed_ref, ss, rs).start()
+
+    def line_sum(part_ref, landed_ref, ss, rs, first):
+        for i in reversed(range(15)):
+            frm = from_z(*LINE[i])
+            remote(part_ref.at[frm], landed_ref.at[frm], ss.at[i], rs.at[i], (frm, c)).wait_recv()
+            out[:, first : first + NARROW] += landed_ref[frm].astype(F32)
+
+    def line_sent(part_ref, landed_ref, ss, rs):
+        for i in range(15):
+            line_copy(i, part_ref, landed_ref, ss, rs).wait_send()
 
     for q in range(4):
         rows = [pt[m : m + 1, cut(q)] for m in range(POS)]
@@ -261,8 +279,9 @@
             score = s_ref[pl.ds(k0, STEP), cut(q)]
             new = []
             for m in range(POS):
-                u = 1.0 + jnp.tanh(score - rows[m])
-                v = u * (2.0 - u)
+                t = jnp.tanh(score - rows[m])
+                u = 1.0 + t
+                v = 1.0 - t * t
                 vi[m, pl.ds(k0, STEP), cut(q)] = v
                 new.append(acc[2 * m] + fold(u))
                 new.append(acc[2 * m + 1] + fold(v))
@@ -274,6 +293,8 @@
             x2s[POS + m : POS + m + 1, cut(q)] = jnp.sum(acc[2 * m + 1], axis=0, keepdims=True)
     exchange(x2s, x2r.at[c], x2_ss, x2_rs, peer_c)
     x2r[c] = x2s[...]
+    exchange(pt.at[:, group], jp.at[r], p_ss, p_rs, peer_r)
+    jp[r] = pt[:, group]
 
     def columns(src, first):
         jt[...] = jnp.transpose(src[...].reshape(ROWS * 8, LANES))
@@ -283,9 +304,6 @@
                 jc[first + n, b * SHARD : (b + 1) * SHARD, :] = jnp.broadcast_to(
                     mine_cols[:, b * 8 + n : b * 8 + n + 1], (SHARD, LANES)
                 )
-
-    arrive(pt.at[:, group], jp, p_ss, p_rs, peer_r, r)
-    columns(jp, 0)
 
     arrive(x2s, x2r, x2_ss, x2_rs, peer_c, c)
     total = jnp.sum(x2r[...], axis=0)
@@ -329,13 +347,47 @@
 
         lax.fori_loop(0, steps, tile_i, 0)
 
+    early_line = a_buf[:, :, BOTH_AT:].reshape(BLOCK, NARROW)
+    early_plane = c_buf[:, :, BOTH_AT:].reshape(BLOCK, NARROW)
+    over_rows = (((0,), (0,)), ((), ()))
+    for h in range(2):
+        rows = slice(256 * h, 256 * h + 256)
+        product = jnp.dot(gi[rows, :], early_line, preferred_element_type=F32)
+        ez_part[8 * h : 8 * h + 8] = product.astype(BF16).reshape(8, SHARD, NARROW)
+
+        @pl.when(r // 8 == h)
+        def _(product=product):
+            z_mine[...] = product.reshape(8, SHARD, NARROW)
+
+    line_start(ez_part, ez_landed, e_ss, e_rs)
+    out[:, BOTH_AT:] = z_mine[r % 8]
+    for h in range(2):
+        rows = slice(256 * h, 256 * h + 256)
+        product = lax.dot_general(gi[:, rows], early_plane, over_rows, preferred_element_type=F32)
+        ep_part[8 * h : 8 * h + 8] = product.astype(BF16).reshape(8, SHARD, NARROW)
+
+        @pl.when(c // 8 == h)
+        def _(product=product):
+            z_mine[...] = product.reshape(8, SHARD, NARROW)
+
+    def early_push(n, carry):
+        to = c ^ (16 - n)
+        remote(ep_part.at[to], ep_landed.at[c], f_ss.at[16 - n], f_rs.at[16 - n], (r, to)).start()
+        return carry
+
+    lax.fori_loop(1, 16, early_push, 0)
+    out[:, BOTH_AT:] += z_mine[c % 8]
+
+    arrive(pt.at[:, group], jp, p_ss, p_rs, peer_r, r)
+    columns(jp, 0)
+
     def slopes(i, carry):
         k0 = pl.multiple_of(i * STEP, STEP)
         for m in range(POS):
             col = jc[m, pl.ds(k0, STEP), :]
             for q in range(4):
-                u = 1.0 + jnp.tanh(s_ref[pl.ds(k0, STEP), cut(q)] - col)
-                vj[m, pl.ds(k0, STEP), cut(q)] = u * (2.0 - u)
+                t = jnp.tanh(s_ref[pl.ds(k0, STEP), cut(q)] - col)
+                vj[m, pl.ds(k0, STEP), cut(q)] = 1.0 - t * t
             where = jc[POS + m, pl.ds(k0, STEP), :].astype(I32)
             jc[POS + m, pl.ds(k0, STEP), :] = jnp.where(
                 where // BLOCK == r, where % BLOCK, -1
@@ -365,7 +417,7 @@
 
     lax.fori_loop(0, steps, tile_j, 0)
 
-    right = a_buf[:, :, BROAD:].reshape(BLOCK, NARROW)
+    right = a_buf[:, :, LINE_AT:BOTH_AT].reshape(BLOCK, NARROW)
     for h in range(2):
         rows = slice(256 * h, 256 * h + 256)
         product = jnp.dot(gi[rows, :], right, preferred_element_type=F32)
@@ -376,18 +428,15 @@
         def _(product=product):
             z_mine[...] = product.reshape(8, SHARD, NARROW)
 
-    for i, o in enumerate(LINE):
-        to = ((z + o[0]) % ZS) * 2 + (core + o[1]) % 2
-        remote(z_part.at[to], z_landed.at[r], h_ss.at[i], h_rs.at[i], (to, c)).start()
+    line_start(z_part, z_landed, h_ss, h_rs)
 
     left = c_buf[:, :, :BROAD].reshape(BLOCK, BROAD)
     wide = 2 * LANES
-    dims = (((0,), (0,)), ((), ()))
     for turn_id in range(2):
         h = (c // 8) ^ (1 - turn_id)
         half = pl.ds(pl.multiple_of(h * wide, wide), wide)
-        product = lax.dot_general(gi[:, half], left, dims, preferred_element_type=F32)
-        product = product + lax.dot_general(gj[:, half], left, dims, preferred_element_type=F32)
+        product = lax.dot_general(gi[:, half], left, over_rows, preferred_element_type=F32)
+        product = product + lax.dot_general(gj[:, half], left, over_rows, preferred_element_type=F32)
         part[pl.ds(h * 8, 8)] = product.astype(BF16).reshape(8, SHARD, BROAD)
         if turn_id == 1:
             mine[...] = product.reshape(8, SHARD, BROAD)
@@ -399,36 +448,40 @@
 
         lax.fori_loop(*((8, 16) if turn_id == 0 else (1, 8)), push, 0)
 
-    out[:, BROAD:] = z_mine[r % 8]
     out[:, :BROAD] = mine[c % 8]
-    for i, o in reversed(list(enumerate(LINE))):
-        frm = from_z(o[0], o[1])
-        remote(z_part.at[frm], z_landed.at[frm], h_ss.at[i], h_rs.at[i], (frm, c)).wait_recv()
-        out[:, BROAD:] += z_landed[frm].astype(F32)
-
-    def gather_sum(o, carry):
-        frm = c ^ o
-        remote(part.at[frm], landed.at[frm], g_ss.at[o], g_rs.at[o], (r, frm)).wait_recv()
-        out[:, :BROAD] += landed[frm].astype(F32)
-        return carry
-
-    lax.fori_loop(1, 16, gather_sum, 0)
-
-    def sent_all(o, carry):
-        frm = c ^ o
-        remote(part.at[frm], landed.at[frm], g_ss.at[o], g_rs.at[o], (r, frm)).wait_send()
-        return carry
-
-    lax.fori_loop(1, 16, sent_all, 0)
-    for i, o in enumerate(LINE):
-        to = ((z + o[0]) % ZS) * 2 + (core + o[1]) % 2
-        remote(z_part.at[to], z_landed.at[r], h_ss.at[i], h_rs.at[i], (to, c)).wait_send()
+    out[:, LINE_AT:BOTH_AT] = z_mine[r % 8]
+
+    def plane_sum(part_ref, landed_ref, ss, rs, first, width):
+        def add(o, carry):
+            frm = c ^ o
+            remote(part_ref.at[frm], landed_ref.at[frm], ss.at[o], rs.at[o], (r, frm)).wait_recv()
+            out[:, first : first + width] += landed_ref[frm].astype(F32)
+            return carry
+
+        lax.fori_loop(1, 16, add, 0)
+
+    def plane_sent(part_ref, landed_ref, ss, rs):
+        def wait(o, carry):
+            frm = c ^ o
+            remote(part_ref.at[frm], landed_ref.at[frm], ss.at[o], rs.at[o], (r, frm)).wait_send()
+            return carry
+
+        lax.fori_loop(1, 16, wait, 0)
+
+    line_sum(ez_part, ez_landed, e_ss, e_rs, BOTH_AT)
+    plane_sum(ep_part, ep_landed, f_ss, f_rs, BOTH_AT, NARROW)
+    line_sent(ez_part, ez_landed, e_ss, e_rs)
+    plane_sent(ep_part, ep_landed, f_ss, f_rs)
     leave(x1s, x1r.at[c], x1_ss, x1_rs, peer_c)
     leave(x2s, x2r.at[c], x2_ss, x2_rs, peer_c)
     leave(pt.at[:, group], jp.at[r], p_ss, p_rs, peer_r)
     leave(we.at[:, group], jw.at[r], w_ss, w_rs, peer_r)
     for copy in sent:
         copy.wait_send()
+    line_sum(z_part, z_landed, h_ss, h_rs, LINE_AT)
+    plane_sum(part, landed, g_ss, g_rs, 0, BROAD)
+    line_sent(z_part, z_landed, h_ss, h_rs)
+    plane_sent(part, landed, g_ss, g_rs)
 
 
 def body(embed, positives, placement):
@@ -452,6 +505,10 @@
             pltpu.VMEM((ROWS, SHARD, NARROW), BF16),
             pltpu.VMEM((ROWS, SHARD, NARROW), BF16),
             pltpu.VMEM((8, SHARD, NARROW), F32),
+            pltpu.VMEM((ROWS, SHARD, NARROW), BF16),
+            pltpu.VMEM((ROWS, SHARD, NARROW), BF16),
+            pltpu.VMEM((COLS, SHARD, NARROW), BF16),
+            pltpu.VMEM((COLS, SHARD, NARROW), BF16),
             pltpu.VMEM((POS, BLOCK), I32),
             pltpu.VMEM((64, LANES), I32),
             pltpu.VMEM((8, BLOCK), I32),
@@ -469,7 +526,7 @@
             dma((24,)),
             dma((24,)),
         ]
-        + [dma((16,))] * 16,
+        + [dma((16,))] * 20,
         compiler_params=pltpu.CompilerParams(
             collective_id=0, has_side_effects=True, vmem_limit_bytes=60 * 1024 * 1024
         ),

time: 62.3 us -> 59.9 us (0.961)
  Pallas kernels: 60.6 us -> 58.2 us
    pallas_call x1, Pallas kernels: 60.6 us -> 58.2 us  [body(): pl.pallas_call(kernel, out_shape=jax.ShapeDtypeStruct((SHARD, WIDTH), F32...]
where the time goes in v3:
time: 59.9 us; the launch traced here: 59.8 us
  Pallas kernels  58.2 us (97%)
  local copies, waits for them, and re-layouts  1.57 us (3%)
    pallas_call x1, Pallas kernels, body(): pl.pallas_call(kernel, out_shape=jax.ShapeDtypeStruct((SHARD, WIDTH), F32...  58.2 us
    unnamed x1, local copies, waits for them, and re-layouts  1.57 us

profile of v3, /device:TPU:1, one launch (start us, length us, event | category | flops | bytes accessed | tf_op | source)
XLA Modules:
  0.0 59.8 jit_solution(3650523356878907168)
XLA Ops:
  0.0 58.2 %smooth_ap.1 = f32[32,1024]{1,0:T(8,128)} custom-call(bf16[32,1024]{1,0:T(8,128)(2,1)} %embed.1, s32[4,512]{1,0:T(4,128)} %bitcast.3, s32[64,128]{1,0:T(8,128)} %bitcast.2), custom_call_target="tpu_custom_call" | custom-call | flops 2147483648 | bytes 4194304 | tf_op jit(solution)/shard_map/smooth_ap/pallas_call | solution.py:489
  58.2 1.6 %copy.5 = f32[32,1024]{1,0:T(8,128)} copy(f32[32,1024]{1,0:T(8,128)} %smooth_ap.1) | data formatting | bytes 262144

commit v4 on v3

--- a/solution.py
+++ b/solution.py
@@ -18,13 +18,12 @@
 LANES = 128
 STEP = 64
 
-BROAD, NARROW = 512, 256
+BROAD, NARROW, EARLY = 384, 256, 384
 LINE_AT, BOTH_AT = BROAD, BROAD + NARROW
 
-LINE = (
-    (4, 0), (3, 1), (5, 0), (4, 1), (3, 0), (5, 1), (2, 0), (6, 1),
-    (2, 1), (6, 0), (1, 0), (7, 1), (1, 1), (7, 0), (0, 1),
-)
+DEPTHS = (4, 3, 5, 2, 6, 1, 7)
+PLANE = (10, 11, 14, 9, 6, 8, 2, 15, 13, 7, 5, 12, 4, 3, 1)
+LINE = (8, 9, 10, 11, 6, 7, 14, 15, 12, 13, 4, 5, 2, 3, 1)
 
 
 def remote(src, dst, send, recv, device):
@@ -36,10 +35,10 @@
 
 def kernel(
     embed, positives, placement, out,
-    a_buf, c_buf, s_ref, vi, vj, gi, gj, part, landed, mine, z_part, z_landed, z_mine,
-    ez_part, ez_landed, ep_part, ep_landed,
+    a_buf, c_buf, s_ref, vi, vj, gi, gj, part, landed, mine, z_part, z_landed, z_whole, z_other,
+    ez_part, ez_landed, e_whole, e_other, ep_part, ep_landed,
     pos_in, place_in, tgt, pt, we, x1s, x1r, x2s, x2r, jp, jw, jt, jc,
-    in_sem, plane_s, plane_r, z_s, z_r, sib_s, sib_r,
+    in_sem, z_sem, e_sem, plane_s, plane_r, z_s, z_r, sib_s, sib_r,
     x1_ss, x1_rs, x2_ss, x2_rs, p_ss, p_rs, w_ss, w_rs, g_ss, g_rs, h_ss, h_rs,
     e_ss, e_rs, f_ss, f_rs,
 ):
@@ -217,12 +216,9 @@
                 acc[m], axis=0, keepdims=True
             )
 
-    def exchange(src, dst, ss, rs, peer):
-        def start(o, carry):
+    def exchange(src, dst, ss, rs, peer, order):
+        for o in order:
             remote(src, dst, ss.at[o], rs.at[o], peer(o)).start()
-            return carry
-
-        lax.fori_loop(1, 16, start, 0)
 
     def arrive(src, dst, ss, rs, peer, index):
         def wait(o, carry):
@@ -244,7 +240,7 @@
     def peer_r(o):
         return (r ^ o, c)
 
-    exchange(x1s, x1r.at[c], x1_ss, x1_rs, peer_c)
+    exchange(x1s, x1r.at[c], x1_ss, x1_rs, peer_c, PLANE)
     x1r[c] = x1s[...]
     arrive(x1s, x1r, x1_ss, x1_rs, peer_c, c)
     total = jnp.sum(x1r[...], axis=0)
@@ -252,24 +248,33 @@
     pt[0:POS, 256:512] = total[POS : 2 * POS]
 
     group = pl.ds(pl.multiple_of(y * LANES, LANES), LANES)
-    def line_copy(i, part_ref, landed_ref, ss, rs):
-        o = LINE[i]
-        to = ((z + o[0]) % ZS) * 2 + (core + o[1]) % 2
-        return remote(part_ref.at[to], landed_ref.at[r], ss.at[i], rs.at[i], (to, c))
-
-    def line_start(part_ref, landed_ref, ss, rs):
-        for i in range(15):
-            line_copy(i, part_ref, landed_ref, ss, rs).start()
-
-    def line_sum(part_ref, landed_ref, ss, rs, first):
-        for i in reversed(range(15)):
-            frm = from_z(*LINE[i])
-            remote(part_ref.at[frm], landed_ref.at[frm], ss.at[i], rs.at[i], (frm, c)).wait_recv()
-            out[:, first : first + NARROW] += landed_ref[frm].astype(F32)
+    def line_meet(tiles, columns, whole, other, sem):
+        for h in range(2):
+            rows = slice(256 * h, 256 * h + 256)
+            product = sum(jnp.dot(g[rows, :], columns, preferred_element_type=F32) for g in tiles)
+            whole[4 * h : 4 * h + 4] = product.reshape(4, 2, SHARD, product.shape[1])
+        remote(whole.at[:, 1 - core], other, sem.at[0], sem.at[1], (r ^ 1, c)).start()
+
+    def line_go(whole, other, part_ref, landed_ref, sem, ss, rs):
+        meet = remote(whole.at[:, 1 - core], other, sem.at[0], sem.at[1], (r ^ 1, c))
+        meet.wait_recv()
+        part_ref[...] = (whole[:, core] + other[...]).astype(BF16)
+        for d in DEPTHS:
+            to = (z + d) % ZS
+            remote(part_ref.at[to], landed_ref.at[z], ss.at[d], rs.at[d], in_line(d)).start()
+        meet.wait_send()
+        return whole[z, core] + other[z]
+
+    def line_sum(landed_ref, ss, rs, first, width):
+        for d in reversed(DEPTHS):
+            frm = (z + ZS - d) % ZS
+            remote(landed_ref.at[frm], landed_ref.at[frm], ss.at[d], rs.at[d], in_line(d)).wait_recv()
+            out[:, first : first + width] += landed_ref[frm].astype(F32)
 
     def line_sent(part_ref, landed_ref, ss, rs):
-        for i in range(15):
-            line_copy(i, part_ref, landed_ref, ss, rs).wait_send()
+        for d in DEPTHS:
+            to = (z + d) % ZS
+            remote(part_ref.at[to], landed_ref.at[z], ss.at[d], rs.at[d], in_line(d)).wait_send()
 
     for q in range(4):
         rows = [pt[m : m + 1, cut(q)] for m in range(POS)]
@@ -291,9 +296,9 @@
         for m in range(POS):
             x2s[m : m + 1, cut(q)] = jnp.sum(acc[2 * m], axis=0, keepdims=True)
             x2s[POS + m : POS + m + 1, cut(q)] = jnp.sum(acc[2 * m + 1], axis=0, keepdims=True)
-    exchange(x2s, x2r.at[c], x2_ss, x2_rs, peer_c)
+    exchange(x2s, x2r.at[c], x2_ss, x2_rs, peer_c, PLANE)
     x2r[c] = x2s[...]
-    exchange(pt.at[:, group], jp.at[r], p_ss, p_rs, peer_r)
+    exchange(pt.at[:, group], jp.at[r], p_ss, p_rs, peer_r, LINE)
     jp[r] = pt[:, group]
 
     def columns(src, first):
@@ -327,7 +332,7 @@
         we[m : m + 1, :] = 0.25 * weight
         we[POS + m : POS + m + 1, :] = pulled[m] - weight * slope[m]
 
-    exchange(we.at[:, group], jw.at[r], w_ss, w_rs, peer_r)
+    exchange(we.at[:, group], jw.at[r], w_ss, w_rs, peer_r, LINE)
     jw[r] = we[:, group]
 
     for q in range(4):
@@ -347,36 +352,22 @@
 
         lax.fori_loop(0, steps, tile_i, 0)
 
-    early_line = a_buf[:, :, BOTH_AT:].reshape(BLOCK, NARROW)
-    early_plane = c_buf[:, :, BOTH_AT:].reshape(BLOCK, NARROW)
     over_rows = (((0,), (0,)), ((), ()))
-    for h in range(2):
-        rows = slice(256 * h, 256 * h + 256)
-        product = jnp.dot(gi[rows, :], early_line, preferred_element_type=F32)
-        ez_part[8 * h : 8 * h + 8] = product.astype(BF16).reshape(8, SHARD, NARROW)
-
-        @pl.when(r // 8 == h)
-        def _(product=product):
-            z_mine[...] = product.reshape(8, SHARD, NARROW)
-
-    line_start(ez_part, ez_landed, e_ss, e_rs)
-    out[:, BOTH_AT:] = z_mine[r % 8]
+    line_meet((gi,), a_buf[:, :, BOTH_AT:].reshape(BLOCK, EARLY), e_whole, e_other, e_sem)
+    early_plane = c_buf[:, :, BOTH_AT:].reshape(BLOCK, EARLY)
     for h in range(2):
         rows = slice(256 * h, 256 * h + 256)
         product = lax.dot_general(gi[:, rows], early_plane, over_rows, preferred_element_type=F32)
-        ep_part[8 * h : 8 * h + 8] = product.astype(BF16).reshape(8, SHARD, NARROW)
+        ep_part[8 * h : 8 * h + 8] = product.astype(BF16).reshape(8, SHARD, EARLY)
 
         @pl.when(c // 8 == h)
         def _(product=product):
-            z_mine[...] = product.reshape(8, SHARD, NARROW)
-
-    def early_push(n, carry):
-        to = c ^ (16 - n)
-        remote(ep_part.at[to], ep_landed.at[c], f_ss.at[16 - n], f_rs.at[16 - n], (r, to)).start()
-        return carry
-
-    lax.fori_loop(1, 16, early_push, 0)
-    out[:, BOTH_AT:] += z_mine[c % 8]
+            mine[...] = product.reshape(8, SHARD, EARLY)
+
+    for o in PLANE:
+        remote(ep_part.at[c ^ o], ep_landed.at[c], f_ss.at[o], f_rs.at[o], (r, c ^ o)).start()
+    out[:, BOTH_AT:] = mine[c % 8]
+    out[:, BOTH_AT:] += line_go(e_whole, e_other, ez_part, ez_landed, e_sem, e_ss, e_rs)
 
     arrive(pt.at[:, group], jp, p_ss, p_rs, peer_r, r)
     columns(jp, 0)
@@ -417,18 +408,7 @@
 
     lax.fori_loop(0, steps, tile_j, 0)
 
-    right = a_buf[:, :, LINE_AT:BOTH_AT].reshape(BLOCK, NARROW)
-    for h in range(2):
-        rows = slice(256 * h, 256 * h + 256)
-        product = jnp.dot(gi[rows, :], right, preferred_element_type=F32)
-        product = product + jnp.dot(gj[rows, :], right, preferred_element_type=F32)
-        z_part[8 * h : 8 * h + 8] = product.astype(BF16).reshape(8, SHARD, NARROW)
-
-        @pl.when(r // 8 == h)
-        def _(product=product):
-            z_mine[...] = product.reshape(8, SHARD, NARROW)
-
-    line_start(z_part, z_landed, h_ss, h_rs)
+    line_meet((gi, gj), a_buf[:, :, LINE_AT:BOTH_AT].reshape(BLOCK, NARROW), z_whole, z_other, z_sem)
 
     left = c_buf[:, :, :BROAD].reshape(BLOCK, BROAD)
     wide = 2 * LANES
@@ -441,15 +421,12 @@
         if turn_id == 1:
             mine[...] = product.reshape(8, SHARD, BROAD)
 
-        def push(n, carry):
-            to = c ^ n
-            remote(part.at[to], landed.at[c], g_ss.at[n], g_rs.at[n], (r, to)).start()
-            return carry
-
-        lax.fori_loop(*((8, 16) if turn_id == 0 else (1, 8)), push, 0)
+        for o in PLANE:
+            if (o < 8) == (turn_id == 1):
+                remote(part.at[c ^ o], landed.at[c], g_ss.at[o], g_rs.at[o], (r, c ^ o)).start()
 
     out[:, :BROAD] = mine[c % 8]
-    out[:, LINE_AT:BOTH_AT] = z_mine[r % 8]
+    out[:, LINE_AT:BOTH_AT] = line_go(z_whole, z_other, z_part, z_landed, z_sem, h_ss, h_rs)
 
     def plane_sum(part_ref, landed_ref, ss, rs, first, width):
         def add(o, carry):
@@ -468,8 +445,8 @@
 
         lax.fori_loop(1, 16, wait, 0)
 
-    line_sum(ez_part, ez_landed, e_ss, e_rs, BOTH_AT)
-    plane_sum(ep_part, ep_landed, f_ss, f_rs, BOTH_AT, NARROW)
+    line_sum(ez_landed, e_ss, e_rs, BOTH_AT, EARLY)
+    plane_sum(ep_part, ep_landed, f_ss, f_rs, BOTH_AT, EARLY)
     line_sent(ez_part, ez_landed, e_ss, e_rs)
     plane_sent(ep_part, ep_landed, f_ss, f_rs)
     leave(x1s, x1r.at[c], x1_ss, x1_rs, peer_c)
@@ -478,7 +455,7 @@
     leave(we.at[:, group], jw.at[r], w_ss, w_rs, peer_r)
     for copy in sent:
         copy.wait_send()
-    line_sum(z_part, z_landed, h_ss, h_rs, LINE_AT)
+    line_sum(z_landed, h_ss, h_rs, LINE_AT, NARROW)
     plane_sum(part, landed, g_ss, g_rs, 0, BROAD)
     line_sent(z_part, z_landed, h_ss, h_rs)
     plane_sent(part, landed, g_ss, g_rs)
@@ -502,13 +479,16 @@
             pltpu.VMEM((COLS, SHARD, BROAD), BF16),
             pltpu.VMEM((COLS, SHARD, BROAD), BF16),
             pltpu.VMEM((8, SHARD, BROAD), F32),
-            pltpu.VMEM((ROWS, SHARD, NARROW), BF16),
-            pltpu.VMEM((ROWS, SHARD, NARROW), BF16),
-            pltpu.VMEM((8, SHARD, NARROW), F32),
-            pltpu.VMEM((ROWS, SHARD, NARROW), BF16),
-            pltpu.VMEM((ROWS, SHARD, NARROW), BF16),
-            pltpu.VMEM((COLS, SHARD, NARROW), BF16),
-            pltpu.VMEM((COLS, SHARD, NARROW), BF16),
+            pltpu.VMEM((ZS, SHARD, NARROW), BF16),
+            pltpu.VMEM((ZS, SHARD, NARROW), BF16),
+            pltpu.VMEM((ZS, 2, SHARD, NARROW), F32),
+            pltpu.VMEM((ZS, SHARD, NARROW), F32),
+            pltpu.VMEM((ZS, SHARD, EARLY), BF16),
+            pltpu.VMEM((ZS, SHARD, EARLY), BF16),
+            pltpu.VMEM((ZS, 2, SHARD, EARLY), F32),
+            pltpu.VMEM((ZS, SHARD, EARLY), F32),
+            pltpu.VMEM((COLS, SHARD, EARLY), BF16),
+            pltpu.VMEM((COLS, SHARD, EARLY), BF16),
             pltpu.VMEM((POS, BLOCK), I32),
             pltpu.VMEM((64, LANES), I32),
             pltpu.VMEM((8, BLOCK), I32),
@@ -523,6 +503,8 @@
             pltpu.VMEM((LANES, LANES), F32),
             pltpu.VMEM((4 * POS, BLOCK, LANES), F32),
             dma((4,)),
+            dma((2,)),
+            dma((2,)),
             dma((24,)),
             dma((24,)),
         ]

time: 59.9 us -> 56.6 us (0.945)
  Pallas kernels: 58.2 us -> 54.8 us
    pallas_call x1, Pallas kernels: 58.2 us -> 54.8 us  [body(): pl.pallas_call(kernel, out_shape=jax.ShapeDtypeStruct((SHARD, WIDTH), F32...]
where the time goes in v4:
time: 56.6 us; the launch traced here: 56.4 us
  Pallas kernels  54.8 us (97%)
  local copies, waits for them, and re-layouts  1.57 us (3%)
    pallas_call x1, Pallas kernels, body(): pl.pallas_call(kernel, out_shape=jax.ShapeDtypeStruct((SHARD, WIDTH), F32...  54.8 us
    unnamed x1, local copies, waits for them, and re-layouts  1.57 us

profile of v4, /device:TPU:1, one launch (start us, length us, event | category | flops | bytes accessed | tf_op | source)
XLA Modules:
  0.0 56.4 jit_solution(14983259093878803769)
XLA Ops:
  0.0 54.8 %smooth_ap.1 = f32[32,1024]{1,0:T(8,128)} custom-call(bf16[32,1024]{1,0:T(8,128)(2,1)} %embed.1, s32[4,512]{1,0:T(4,128)} %bitcast.3, s32[64,128]{1,0:T(8,128)} %bitcast.2), custom_call_target="tpu_custom_call" | custom-call | flops 2147483648 | bytes 4194304 | tf_op jit(solution)/shard_map/smooth_ap/pallas_call | solution.py:466
  54.9 1.6 %copy.5 = f32[32,1024]{1,0:T(8,128)} copy(f32[32,1024]{1,0:T(8,128)} %smooth_ap.1) | data formatting | bytes 262144

commit v5 on v4

--- a/solution.py
+++ b/solution.py
@@ -62,15 +62,13 @@
         load.start()
     barrier = pltpu.get_barrier_semaphore()
 
-    def greet(o, carry):
-        pl.semaphore_signal(barrier, inc=1, device_id=(r, c ^ o), device_id_type=MESH)
-        pl.semaphore_signal(barrier, inc=1, device_id=(r ^ o, c), device_id_type=MESH)
-        return carry
-
-    lax.fori_loop(1, 16, greet, 0)
+    near = [in_line(2), in_line(6), in_plane((0, 2)), in_plane((2, 0)), in_line(1), in_line(7)]
+    near += [in_plane((0, 1)), in_plane((1, 0)), in_plane((0, 3)), in_plane((3, 0)), in_line(0, 1)]
+    for peer in near:
+        pl.semaphore_signal(barrier, inc=1, device_id=peer, device_id_type=MESH)
     for load in loads:
         load.wait()
-    pl.semaphore_wait(barrier, 30)
+    pl.semaphore_wait(barrier, len(near))
 
     sent = []
 

time: 56.6 us -> 55.2 us (0.975)
  Pallas kernels: 54.8 us -> 53.4 us
    pallas_call x1, Pallas kernels: 54.8 us -> 53.4 us  [body(): pl.pallas_call(kernel, out_shape=jax.ShapeDtypeStruct((SHARD, WIDTH), F32...]
where the time goes in v5:
time: 55.2 us; the launch traced here: 55 us
  Pallas kernels  53.4 us (97%)
  local copies, waits for them, and re-layouts  1.57 us (3%)
    pallas_call x1, Pallas kernels, body(): pl.pallas_call(kernel, out_shape=jax.ShapeDtypeStruct((SHARD, WIDTH), F32...  53.4 us
    unnamed x1, local copies, waits for them, and re-layouts  1.57 us

profile of v5, /device:TPU:1, one launch (start us, length us, event | category | flops | bytes accessed | tf_op | source)
XLA Modules:
  0.0 55.0 jit_solution(14030545234869613690)
XLA Ops:
  0.0 53.4 %smooth_ap.1 = f32[32,1024]{1,0:T(8,128)} custom-call(bf16[32,1024]{1,0:T(8,128)(2,1)} %embed.1, s32[4,512]{1,0:T(4,128)} %bitcast.3, s32[64,128]{1,0:T(8,128)} %bitcast.2), custom_call_target="tpu_custom_call" | custom-call | flops 2147483648 | bytes 4194304 | tf_op jit(solution)/shard_map/smooth_ap/pallas_call | solution.py:464
  53.4 1.6 %copy.5 = f32[32,1024]{1,0:T(8,128)} copy(f32[32,1024]{1,0:T(8,128)} %smooth_ap.1) | data formatting | bytes 262144

commit v6 on v5

--- a/solution.py
+++ b/solution.py
@@ -18,7 +18,7 @@
 LANES = 128
 STEP = 64
 
-BROAD, NARROW, EARLY = 384, 256, 384
+BROAD, NARROW, EARLY = 256, 256, 512
 LINE_AT, BOTH_AT = BROAD, BROAD + NARROW
 
 DEPTHS = (4, 3, 5, 2, 6, 1, 7)
@@ -36,7 +36,7 @@
 def kernel(
     embed, positives, placement, out,
     a_buf, c_buf, s_ref, vi, vj, gi, gj, part, landed, mine, z_part, z_landed, z_whole, z_other,
-    ez_part, ez_landed, e_whole, e_other, ep_part, ep_landed,
+    ez_part, ez_landed, e_whole, e_other, ep_part, ep_landed, e_mine,
     pos_in, place_in, tgt, pt, we, x1s, x1r, x2s, x2r, jp, jw, jt, jc,
     in_sem, z_sem, e_sem, plane_s, plane_r, z_s, z_r, sib_s, sib_r,
     x1_ss, x1_rs, x2_ss, x2_rs, p_ss, p_rs, w_ss, w_rs, g_ss, g_rs, h_ss, h_rs,
@@ -108,15 +108,26 @@
         remote(view, view, sib_s.at[slot], sib_r.at[slot], in_line(0, 1)).wait_recv()
 
     every, top, low_half = pl.ds(0, SHARD), pl.ds(0, SHARD // 2), pl.ds(SHARD // 2, SHARD // 2)
-    z_send(2, r, every, 2, 2)
-    z_send(-2, r, every, -2, 6)
-    a_send(c, every, 0, 2, 1)
-    a_send(c, every, 2, 0, 4)
-    z_send(1, r, every, 1, 1)
-    z_send(-1, r, every, -1, 7)
-    for d in (1, 3):
-        a_send(c, every, 0, d, d - 1)
-        a_send(c, every, d, 0, d + 2)
+    halves = (top, low_half)
+
+    def x_first(d, h):
+        a_send(c, halves[h], 0, d, 4 * d - 4 + h)
+
+    def y_first(d, h):
+        a_send(c, halves[h], d, 0, 4 * d - 2 + h)
+
+    for d in (2, 1, 3):
+        x_first(d, 0)
+        y_first(d, 1)
+    z_send(2, r, top, 2, 0)
+    z_send(-2, r, low_half, -2, 1)
+    z_send(2, r, low_half, 2, 2)
+    z_send(-2, r, top, -2, 3)
+    z_send(1, r, every, 1, 4)
+    z_send(-1, r, every, -1, 5)
+    for d in (2, 1, 3):
+        x_first(d, 1)
+        y_first(d, 0)
     sib_send(0, every, 0)
 
     table = place_in[...]
@@ -137,38 +148,48 @@
         tgt[m : m + 1, :] = jnp.where(here, (where // BLOCK) * SHARD + where % SHARD, -1)
 
     def turn(d):
-        a_wait(0, d, every, d - 1)
+        a_wait(0, d, top, 4 * d - 4)
         for e in (2, 1, 3):
-            a_send(from_plane(0, d), top, e, 0, 6 + 3 * (d - 1) + e - 1)
-        a_wait(d, 0, every, d + 2)
+            a_send(from_plane(0, d), top, e, 0, 12 + 3 * (d - 1) + e - 1)
+        a_wait(d, 0, low_half, 4 * d - 1)
         for e in (2, 1, 3):
-            a_send(from_plane(d, 0), low_half, 0, e, 15 + 3 * (d - 1) + e - 1)
+            a_send(from_plane(d, 0), low_half, 0, e, 21 + 3 * (d - 1) + e - 1)
 
     turn(1)
     turn(3)
-    z_wait(2, every, 2)
-    z_send(4, from_z(2), top, 2, 4)
-    z_send(3, from_z(2), every, 1, 3)
-    z_wait(-2, every, 6)
+    z_wait(2, top, 0)
+    z_send(4, from_z(2), top, 2, 6)
+    z_send(3, from_z(2), top, 1, 7)
+    z_wait(-2, low_half, 1)
     z_send(-4, from_z(-2), low_half, -2, 8)
-    z_send(-3, from_z(-2), every, -1, 5)
+    z_send(-3, from_z(-2), low_half, -1, 9)
+    z_wait(2, low_half, 2)
+    z_send(3, from_z(2), low_half, 1, 10)
+    z_wait(-2, top, 3)
+    z_send(-3, from_z(-2), top, -1, 11)
     turn(2)
     for d, slot in ((2, 2), (-2, 6)):
         sib_send(d, every, slot)
-    for d, slot in ((1, 1), (-1, 7)):
+    for d, slot in ((1, 4), (-1, 5)):
         z_wait(d, every, slot)
-        sib_send(d, every, slot)
-    for d, slot in ((3, 3), (-3, 5)):
-        z_wait(d, every, slot)
-        sib_send(d, every, slot)
-    z_wait(4, top, 4)
+        sib_send(d, every, 1 if d == 1 else 7)
+    z_wait(4, top, 6)
     sib_send(4, top, 4)
     z_wait(-4, low_half, 8)
     sib_send(-4, low_half, 8)
+    z_wait(3, top, 7)
+    z_wait(3, low_half, 10)
+    sib_send(3, every, 3)
+    z_wait(-3, low_half, 9)
+    z_wait(-3, top, 11)
+    sib_send(-3, every, 5)
+    for d in (1, 3, 2):
+        a_wait(0, d, low_half, 4 * d - 3)
+        a_wait(d, 0, top, 4 * d - 2)
     for d in (1, 3, 2):
         for e in (1, 3, 2):
-            a_wait(e, d, top, 6 + 3 * (d - 1) + e - 1)
-            a_wait(d, e, low_half, 15 + 3 * (d - 1) + e - 1)
+            a_wait(e, d, top, 12 + 3 * (d - 1) + e - 1)
+            a_wait(d, e, low_half, 21 + 3 * (d - 1) + e - 1)
     for d, slot in ((0, 0), (1, 1), (-1, 7), (2, 2), (-2, 6), (3, 3), (-3, 5)):
         sib_wait(d, every, slot)
     sib_wait(4, top, 4)
@@ -360,15 +381,15 @@
 
         @pl.when(c // 8 == h)
         def _(product=product):
-            mine[...] = product.reshape(8, SHARD, EARLY)
+            e_mine[...] = product.reshape(8, SHARD, EARLY)
 
     for o in PLANE:
         remote(ep_part.at[c ^ o], ep_landed.at[c], f_ss.at[o], f_rs.at[o], (r, c ^ o)).start()
-    out[:, BOTH_AT:] = mine[c % 8]
-    out[:, BOTH_AT:] += line_go(e_whole, e_other, ez_part, ez_landed, e_sem, e_ss, e_rs)
+    out[:, BOTH_AT:] = e_mine[c % 8]
 
     arrive(pt.at[:, group], jp, p_ss, p_rs, peer_r, r)
     columns(jp, 0)
+    out[:, BOTH_AT:] += line_go(e_whole, e_other, ez_part, ez_landed, e_sem, e_ss, e_rs)
 
     def slopes(i, carry):
         k0 = pl.multiple_of(i * STEP, STEP)
@@ -389,22 +410,22 @@
     columns(jw, 2 * POS)
 
     def tile_j(i, carry):
-        k0 = pl.multiple_of(i * STEP, STEP)
-        for q in range(4):
-            dense = jc[2 * POS, pl.ds(k0, STEP), :] * vj[0, pl.ds(k0, STEP), cut(q)]
-            for m in range(1, POS):
-                dense = dense + jc[2 * POS + m, pl.ds(k0, STEP), :] * vj[m, pl.ds(k0, STEP), cut(q)]
-            lane = (iota_a + q * LANES).astype(F32)
-            for m in range(POS):
-                dense = dense + jnp.where(
-                    jc[POS + m, pl.ds(k0, STEP), :] == lane,
-                    jc[3 * POS + m, pl.ds(k0, STEP), :],
-                    0.0,
-                )
-            gj[pl.ds(k0, STEP), cut(q)] = dense.astype(BF16)
+        for part_id in range(2):
+            k0 = pl.ds(pl.multiple_of(i * 32 + part_id * 16, 16), 16)
+            weights = [jc[2 * POS + m, k0, :] for m in range(POS)]
+            extras = [jc[3 * POS + m, k0, :] for m in range(POS)]
+            at = [jc[POS + m, k0, :] for m in range(POS)]
+            for q in range(4):
+                dense = weights[0] * vj[0, k0, cut(q)]
+                for m in range(1, POS):
+                    dense = dense + weights[m] * vj[m, k0, cut(q)]
+                lane = (iota_a[0:16, :] + q * LANES).astype(F32)
+                for m in range(POS):
+                    dense = dense + jnp.where(at[m] == lane, extras[m], 0.0)
+                gj[k0, cut(q)] = dense.astype(BF16)
         return carry
 
-    lax.fori_loop(0, steps, tile_j, 0)
+    lax.fori_loop(0, BLOCK // 32, tile_j, 0)
 
     line_meet((gi, gj), a_buf[:, :, LINE_AT:BOTH_AT].reshape(BLOCK, NARROW), z_whole, z_other, z_sem)
 
@@ -487,6 +508,7 @@
             pltpu.VMEM((ZS, SHARD, EARLY), F32),
             pltpu.VMEM((COLS, SHARD, EARLY), BF16),
             pltpu.VMEM((COLS, SHARD, EARLY), BF16),
+            pltpu.VMEM((8, SHARD, EARLY), F32),
             pltpu.VMEM((POS, BLOCK), I32),
             pltpu.VMEM((64, LANES), I32),
             pltpu.VMEM((8, BLOCK), I32),
@@ -503,8 +525,8 @@
             dma((4,)),
             dma((2,)),
             dma((2,)),
-            dma((24,)),
-            dma((24,)),
+            dma((32,)),
+            dma((32,)),
         ]
         + [dma((16,))] * 20,
         compiler_params=pltpu.CompilerParams(

time: 55.2 us -> 53.2 us (0.964)
  Pallas kernels: 53.4 us -> 51.4 us
    pallas_call x1, Pallas kernels: 53.4 us -> 51.4 us  [body(): pl.pallas_call(kernel, out_shape=jax.ShapeDtypeStruct((SHARD, WIDTH), F32...]
where the time goes in v6:
time: 53.2 us; the launch traced here: 53 us
  Pallas kernels  51.4 us (97%)
  local copies, waits for them, and re-layouts  1.57 us (3%)
    pallas_call x1, Pallas kernels, body(): pl.pallas_call(kernel, out_shape=jax.ShapeDtypeStruct((SHARD, WIDTH), F32...  51.4 us
    unnamed x1, local copies, waits for them, and re-layouts  1.57 us

profile of v6, /device:TPU:1, one launch (start us, length us, event | category | flops | bytes accessed | tf_op | source)
XLA Modules:
  0.0 53.0 jit_solution(18144167228476668984)
XLA Ops:
  0.0 51.4 %smooth_ap.1 = f32[32,1024]{1,0:T(8,128)} custom-call(bf16[32,1024]{1,0:T(8,128)(2,1)} %embed.1, s32[4,512]{1,0:T(4,128)} %bitcast.3, s32[64,128]{1,0:T(8,128)} %bitcast.2), custom_call_target="tpu_custom_call" | custom-call | flops 2147483648 | bytes 4194304 | tf_op jit(solution)/shard_map/smooth_ap/pallas_call | solution.py:485
  51.4 1.6 %copy.5 = f32[32,1024]{1,0:T(8,128)} copy(f32[32,1024]{1,0:T(8,128)} %smooth_ap.1) | data formatting | bytes 262144

commit v7 on v6

--- a/solution.py
+++ b/solution.py
@@ -230,10 +230,7 @@
 
         acc = lax.fori_loop(0, steps, pick, (jnp.zeros((8, LANES), F32),) * POS)
         for m in range(POS):
-            half, lane = q // 2, (q % 2) * LANES
-            x1s[half * POS + m : half * POS + m + 1, lane : lane + LANES] = jnp.sum(
-                acc[m], axis=0, keepdims=True
-            )
+            x1s[m * POS + q : m * POS + q + 1, :] = jnp.sum(acc[m], axis=0, keepdims=True)
 
     def exchange(src, dst, ss, rs, peer, order):
         for o in order:
@@ -262,9 +259,10 @@
     exchange(x1s, x1r.at[c], x1_ss, x1_rs, peer_c, PLANE)
     x1r[c] = x1s[...]
     arrive(x1s, x1r, x1_ss, x1_rs, peer_c, c)
-    total = jnp.sum(x1r[...], axis=0)
-    pt[0:POS, 0:256] = total[0:POS]
-    pt[0:POS, 256:512] = total[POS : 2 * POS]
+    scores = jnp.sum(x1r[...], axis=0)
+    for m in range(POS):
+        for q in range(4):
+            pt[m : m + 1, cut(q)] = scores[m * POS + q : m * POS + q + 1, :]
 
     group = pl.ds(pl.multiple_of(y * LANES, LANES), LANES)
     def line_meet(tiles, columns, whole, other, sem):
@@ -313,8 +311,9 @@
 
         acc = lax.fori_loop(0, steps, count, (jnp.zeros((8, LANES), F32),) * (2 * POS))
         for m in range(POS):
-            x2s[m : m + 1, cut(q)] = jnp.sum(acc[2 * m], axis=0, keepdims=True)
-            x2s[POS + m : POS + m + 1, cut(q)] = jnp.sum(acc[2 * m + 1], axis=0, keepdims=True)
+            at = m * POS + q
+            x2s[at : at + 1, :] = jnp.sum(acc[2 * m], axis=0, keepdims=True)
+            x2s[16 + at : 17 + at, :] = jnp.sum(acc[2 * m + 1], axis=0, keepdims=True)
     exchange(x2s, x2r.at[c], x2_ss, x2_rs, peer_c, PLANE)
     x2r[c] = x2s[...]
     exchange(pt.at[:, group], jp.at[r], p_ss, p_rs, peer_r, LINE)
@@ -332,12 +331,16 @@
     arrive(x2s, x2r, x2_ss, x2_rs, peer_c, c)
     total = jnp.sum(x2r[...], axis=0)
     factor = 1.0 / (POS * SHARD * ROWS * COLS)
-    p = [pt[m : m + 1, :] for m in range(POS)]
-    rank = [0.5 + 0.5 * total[m : m + 1] for m in range(POS)]
-    slope = [0.25 * total[POS + m : POS + m + 1] for m in range(POS)]
-    prank = [jnp.full((1, BLOCK), 1.0, F32) for _ in range(POS)]
+
+    def of(value, m):
+        return value[m * POS : (m + 1) * POS]
+
+    p = [of(scores, m) for m in range(POS)]
+    rank = [0.5 + 0.5 * of(total[0:16], m) for m in range(POS)]
+    slope = [0.25 * of(total[16:32], m) for m in range(POS)]
+    prank = [jnp.full((POS, LANES), 1.0, F32) for _ in range(POS)]
     grad = [-factor / rank[m] for m in range(POS)]
-    pulled = [jnp.zeros((1, BLOCK), F32) for _ in range(POS)]
+    pulled = [jnp.zeros((POS, LANES), F32) for _ in range(POS)]
     for m in range(POS):
         for n in range(m + 1, POS):
             t = jnp.tanh(p[n] - p[m])
@@ -348,8 +351,10 @@
             pulled[n] = pulled[n] - pair
     for m in range(POS):
         weight = prank[m] / (rank[m] * rank[m]) * factor / TAU
-        we[m : m + 1, :] = 0.25 * weight
-        we[POS + m : POS + m + 1, :] = pulled[m] - weight * slope[m]
+        quarter, extra = 0.25 * weight, pulled[m] - weight * slope[m]
+        for q in range(4):
+            we[m : m + 1, cut(q)] = quarter[q : q + 1, :]
+            we[POS + m : POS + m + 1, cut(q)] = extra[q : q + 1, :]
 
     exchange(we.at[:, group], jw.at[r], w_ss, w_rs, peer_r, LINE)
     jw[r] = we[:, group]
@@ -484,7 +489,7 @@
     dma = pltpu.SemaphoreType.DMA
     return pl.pallas_call(
         kernel,
-        out_shape=jax.ShapeDtypeStruct((SHARD, WIDTH), F32),
+        out_shape=pltpu.VMEM((SHARD, WIDTH), F32),
         in_specs=[pl.BlockSpec(memory_space=pl.ANY)] * 3,
         out_specs=pl.BlockSpec(memory_space=pltpu.VMEM),
         scratch_shapes=[
@@ -514,10 +519,10 @@
             pltpu.VMEM((8, BLOCK), I32),
             pltpu.VMEM((8, BLOCK), F32),
             pltpu.VMEM((8, BLOCK), F32),
-            pltpu.VMEM((8, BLOCK // 2), F32),
-            pltpu.VMEM((COLS, 8, BLOCK // 2), F32),
-            pltpu.VMEM((8, BLOCK), F32),
-            pltpu.VMEM((COLS, 8, BLOCK), F32),
+            pltpu.VMEM((16, LANES), F32),
+            pltpu.VMEM((COLS, 16, LANES), F32),
+            pltpu.VMEM((32, LANES), F32),
+            pltpu.VMEM((COLS, 32, LANES), F32),
             pltpu.VMEM((ROWS, 8, LANES), F32),
             pltpu.VMEM((ROWS, 8, LANES), F32),
             pltpu.VMEM((LANES, LANES), F32),

time: 53.2 us -> 51.6 us (0.970)
  local copies, waits for them, and re-layouts: 1.57 us -> 0.66 us
  Pallas kernels: 51.4 us -> 50.8 us
    unnamed x1, local copies, waits for them, and re-layouts: 1.57 us -> 0.66 us
    pallas_call x1, Pallas kernels: 51.4 us -> 50.8 us  [body(): pl.pallas_call(kernel, out_shape=pltpu.VMEM((SHARD, WIDTH), F32), in_spec...]
where the time goes in v7:
time: 51.6 us; the launch traced here: 51.4 us
  Pallas kernels  50.8 us (98%)
  local copies, waits for them, and re-layouts  0.66 us (1%)
    pallas_call x1, Pallas kernels, body(): pl.pallas_call(kernel, out_shape=pltpu.VMEM((SHARD, WIDTH), F32), in_spec...  50.8 us

profile of v7, /device:TPU:1, one launch (start us, length us, event | category | flops | bytes accessed | tf_op | source)
XLA Modules:
  0.0 51.4 jit_solution(10061351506760248741)
XLA Ops:
  0.0 50.8 %smooth_ap.1 = f32[32,1024]{1,0:T(8,128)S(1)} custom-call(bf16[32,1024]{1,0:T(8,128)(2,1)} %embed.1, s32[4,512]{1,0:T(4,128)} %bitcast.3, s32[64,128]{1,0:T(8,128)} %bitcast.2), custom_call_target="tpu_custom_call" | custom-call | flops 2147483648 | bytes 4194304 | tf_op jit(solution)/shard_map/smooth_ap/pallas_call | solution.py:490
  50.8 0.7 %copy.5 = f32[32,1024]{1,0:T(8,128)} copy(f32[32,1024]{1,0:T(8,128)S(1)} %smooth_ap.1) | data formatting | bytes 262144

commit v8 on v7

--- a/solution.py
+++ b/solution.py
@@ -58,14 +58,14 @@
         pltpu.make_async_copy(positives, pos_in, in_sem.at[2]),
         pltpu.make_async_copy(placement, place_in, in_sem.at[3]),
     ]
-    for load in loads:
-        load.start()
     barrier = pltpu.get_barrier_semaphore()
 
     near = [in_line(2), in_line(6), in_plane((0, 2)), in_plane((2, 0)), in_line(1), in_line(7)]
     near += [in_plane((0, 1)), in_plane((1, 0)), in_plane((0, 3)), in_plane((3, 0)), in_line(0, 1)]
     for peer in near:
         pl.semaphore_signal(barrier, inc=1, device_id=peer, device_id_type=MESH)
+    for load in loads:
+        load.start()
     for load in loads:
         load.wait()
     pl.semaphore_wait(barrier, len(near))
@@ -190,47 +190,59 @@
         for e in (1, 3, 2):
             a_wait(e, d, top, 12 + 3 * (d - 1) + e - 1)
             a_wait(d, e, low_half, 21 + 3 * (d - 1) + e - 1)
-    for d, slot in ((0, 0), (1, 1), (-1, 7), (2, 2), (-2, 6), (3, 3), (-3, 5)):
+    anchors = a_buf[...].reshape(BLOCK, WIDTH)
+    iota_k = lax.broadcasted_iota(I32, (STEP, LANES), 0)
+    iota_a = lax.broadcasted_iota(I32, (STEP, LANES), 1)
+    steps = BLOCK // STEP
+
+    def fold(value):
+        return jnp.sum(value.reshape(STEP // 8, 8, LANES), axis=0)
+
+    def cut(q):
+        return slice(q * LANES, (q + 1) * LANES)
+
+    def score(first, last):
+        chips = [(z + i) % ZS for i in range(first, last)]
+        cand = jnp.concatenate([c_buf[pl.ds(2 * chip, 2)].reshape(STEP, WIDTH) for chip in chips], axis=0)
+        product = HALF * lax.dot_general(
+            cand, anchors, (((1,), (1,)), ((), ())), preferred_element_type=F32
+        )
+        for i, chip in enumerate(chips):
+            s_ref[pl.ds(pl.multiple_of(chip * STEP, STEP), STEP), :] = product[i * STEP : (i + 1) * STEP]
+
+    def pick(first, last, sums):
+        new = []
+        for q in range(4):
+            rows = [tgt[m : m + 1, cut(q)] for m in range(POS)]
+
+            def step(i, acc, q=q, rows=rows):
+                k0 = pl.multiple_of(((z + i) % ZS) * STEP, STEP)
+                tile = s_ref[pl.ds(k0, STEP), cut(q)]
+                return tuple(
+                    acc[m] + fold(jnp.where(iota_k == rows[m] - k0, tile, 0.0)) for m in range(POS)
+                )
+
+            new.append(lax.fori_loop(first, last, step, sums[q]))
+        return new
+
+    for d, slot in ((0, 0), (1, 1), (-1, 7), (2, 2), (-2, 6)):
+        sib_wait(d, every, slot)
+    score(6, 11)
+    own_rows = pl.ds(pl.multiple_of(r * SHARD, SHARD), SHARD)
+    own_lanes = pl.ds(pl.multiple_of(y * LANES, LANES), LANES)
+    me_row = lax.broadcasted_iota(I32, (SHARD, LANES), 0)
+    me_lane = lax.broadcasted_iota(I32, (SHARD, LANES), 1)
+    s_ref[own_rows, own_lanes] = jnp.where(me_lane - x * SHARD == me_row, -1e30, s_ref[own_rows, own_lanes])
+    sums = pick(6, 11, [(jnp.zeros((8, LANES), F32),) * POS] * 4)
+    for d, slot in ((3, 3), (-3, 5)):
         sib_wait(d, every, slot)
     sib_wait(4, top, 4)
     sib_wait(-4, low_half, 8)
-
-    anchors = a_buf[...].reshape(BLOCK, WIDTH)
-    for h in range(2):
-        cand = c_buf[8 * h : 8 * h + 8].reshape(BLOCK // 2, WIDTH)
-        s_ref[256 * h : 256 * h + 256, :] = HALF * lax.dot_general(
-            cand, anchors, (((1,), (1,)), ((), ())), preferred_element_type=F32
-        )
-    tile = s_ref[pl.ds(pl.multiple_of(r * SHARD, SHARD), SHARD), pl.ds(pl.multiple_of(y * LANES, LANES), LANES)]
-    me_row = lax.broadcasted_iota(I32, (SHARD, LANES), 0)
-    me_lane = lax.broadcasted_iota(I32, (SHARD, LANES), 1)
-    s_ref[pl.ds(pl.multiple_of(r * SHARD, SHARD), SHARD), pl.ds(pl.multiple_of(y * LANES, LANES), LANES)] = (
-        jnp.where(me_lane - x * SHARD == me_row, -1e30, tile)
-    )
-
-    iota_k = lax.broadcasted_iota(I32, (STEP, LANES), 0)
-    iota_a = lax.broadcasted_iota(I32, (STEP, LANES), 1)
-    steps = BLOCK // STEP
-
-    def fold(value):
-        return jnp.sum(value.reshape(STEP // 8, 8, LANES), axis=0)
-
-    def cut(q):
-        return slice(q * LANES, (q + 1) * LANES)
-
+    score(3, 6)
+    sums = pick(3, 6, sums)
     for q in range(4):
-        rows = [tgt[m : m + 1, cut(q)] for m in range(POS)]
-
-        def pick(i, acc, q=q, rows=rows):
-            k0 = pl.multiple_of(i * STEP, STEP)
-            score = s_ref[pl.ds(k0, STEP), cut(q)]
-            return tuple(
-                acc[m] + fold(jnp.where(iota_k == rows[m] - k0, score, 0.0)) for m in range(POS)
-            )
-
-        acc = lax.fori_loop(0, steps, pick, (jnp.zeros((8, LANES), F32),) * POS)
         for m in range(POS):
-            x1s[m * POS + q : m * POS + q + 1, :] = jnp.sum(acc[m], axis=0, keepdims=True)
+            x1s[m * POS + q : m * POS + q + 1, :] = jnp.sum(sums[q][m], axis=0, keepdims=True)
 
     def exchange(src, dst, ss, rs, peer, order):
         for o in order:
@@ -369,8 +381,10 @@
             dense = weights[0] * vi[0, pl.ds(k0, STEP), cut(q)]
             for m in range(1, POS):
                 dense = dense + weights[m] * vi[m, pl.ds(k0, STEP), cut(q)]
-            for m in range(POS):
-                dense = dense + jnp.where(iota_k == rows[m] - k0, extras[m], 0.0)
+            extra = jnp.where(iota_k == rows[0] - k0, extras[0], 0.0)
+            for m in range(1, POS):
+                extra = jnp.where(iota_k == rows[m] - k0, extras[m], extra)
+            dense = dense + extra
             gi[pl.ds(k0, STEP), cut(q)] = dense.astype(BF16)
             return carry
 
@@ -425,8 +439,10 @@
                 for m in range(1, POS):
                     dense = dense + weights[m] * vj[m, k0, cut(q)]
                 lane = (iota_a[0:16, :] + q * LANES).astype(F32)
-                for m in range(POS):
-                    dense = dense + jnp.where(at[m] == lane, extras[m], 0.0)
+                extra = jnp.where(at[0] == lane, extras[0], 0.0)
+                for m in range(1, POS):
+                    extra = jnp.where(at[m] == lane, extras[m], extra)
+                dense = dense + extra
                 gj[k0, cut(q)] = dense.astype(BF16)
         return carry
 

time: 51.6 us -> 51.4 us (level)
  no operation moved by 1% of the time
where the time goes in v8:
time: 51.4 us; the launch traced here: 51.3 us
  Pallas kernels  50.7 us (99%)
  local copies, waits for them, and re-layouts  0.66 us (1%)
    pallas_call x1, Pallas kernels, body(): pl.pallas_call(kernel, out_shape=pltpu.VMEM((SHARD, WIDTH), F32), in_spec...  50.7 us

profile of v8, /device:TPU:1, one launch (start us, length us, event | category | flops | bytes accessed | tf_op | source)
XLA Modules:
  0.0 51.3 jit_solution(6124433540597082894)
XLA Ops:
  0.0 50.7 %smooth_ap.1 = f32[32,1024]{1,0:T(8,128)S(1)} custom-call(bf16[32,1024]{1,0:T(8,128)(2,1)} %embed.1, s32[4,512]{1,0:T(4,128)} %bitcast.3, s32[64,128]{1,0:T(8,128)} %bitcast.2), custom_call_target="tpu_custom_call" | custom-call | flops 2147483648 | bytes 4194304 | tf_op jit(solution)/shard_map/smooth_ap/pallas_call | solution.py:506
  50.7 0.7 %copy.5 = f32[32,1024]{1,0:T(8,128)} copy(f32[32,1024]{1,0:T(8,128)S(1)} %smooth_ap.1) | data formatting | bytes 262144

commit v9 on v8

--- a/solution.py
+++ b/solution.py
@@ -18,7 +18,7 @@
 LANES = 128
 STEP = 64
 
-BROAD, NARROW, EARLY = 256, 256, 512
+BROAD, NARROW, EARLY = 384, 256, 384
 LINE_AT, BOTH_AT = BROAD, BROAD + NARROW
 
 DEPTHS = (4, 3, 5, 2, 6, 1, 7)

time: 51.4 us -> 51.5 us (level)
  no operation moved by 1% of the time
where the time goes in v9:
time: 51.5 us; the launch traced here: 51.3 us
  Pallas kernels  50.7 us (98%)
  local copies, waits for them, and re-layouts  0.66 us (1%)
    pallas_call x1, Pallas kernels, body(): pl.pallas_call(kernel, out_shape=pltpu.VMEM((SHARD, WIDTH), F32), in_spec...  50.7 us

profile of v9, /device:TPU:1, one launch (start us, length us, event | category | flops | bytes accessed | tf_op | source)
XLA Modules:
  0.0 51.3 jit_solution(7178329556757789274)
XLA Ops:
  0.0 50.7 %smooth_ap.1 = f32[32,1024]{1,0:T(8,128)S(1)} custom-call(bf16[32,1024]{1,0:T(8,128)(2,1)} %embed.1, s32[4,512]{1,0:T(4,128)} %bitcast.3, s32[64,128]{1,0:T(8,128)} %bitcast.2), custom_call_target="tpu_custom_call" | custom-call | flops 2147483648 | bytes 4194304 | tf_op jit(solution)/shard_map/smooth_ap/pallas_call | solution.py:506
  50.7 0.7 %copy.5 = f32[32,1024]{1,0:T(8,128)} copy(f32[32,1024]{1,0:T(8,128)S(1)} %smooth_ap.1) | data formatting | bytes 262144

commit v10 on v8

--- a/solution.py
+++ b/solution.py
@@ -295,7 +295,7 @@
         return whole[z, core] + other[z]
 
     def line_sum(landed_ref, ss, rs, first, width):
-        for d in reversed(DEPTHS):
+        for d in DEPTHS:
             frm = (z + ZS - d) % ZS
             remote(landed_ref.at[frm], landed_ref.at[frm], ss.at[d], rs.at[d], in_line(d)).wait_recv()
             out[:, first : first + width] += landed_ref[frm].astype(F32)
@@ -469,13 +469,10 @@
     out[:, LINE_AT:BOTH_AT] = line_go(z_whole, z_other, z_part, z_landed, z_sem, h_ss, h_rs)
 
     def plane_sum(part_ref, landed_ref, ss, rs, first, width):
-        def add(o, carry):
+        for o in PLANE:
             frm = c ^ o
             remote(part_ref.at[frm], landed_ref.at[frm], ss.at[o], rs.at[o], (r, frm)).wait_recv()
             out[:, first : first + width] += landed_ref[frm].astype(F32)
-            return carry
-
-        lax.fori_loop(1, 16, add, 0)
 
     def plane_sent(part_ref, landed_ref, ss, rs):
         def wait(o, carry):

time: 51.4 us -> 51.4 us (level)
  no operation moved by 1% of the time
where the time goes in v10:
time: 51.4 us; the launch traced here: 51.3 us
  Pallas kernels  50.6 us (98%)
  local copies, waits for them, and re-layouts  0.66 us (1%)
    pallas_call x1, Pallas kernels, body(): pl.pallas_call(kernel, out_shape=pltpu.VMEM((SHARD, WIDTH), F32), in_spec...  50.6 us

profile of v10, /device:TPU:1, one launch (start us, length us, event | category | flops | bytes accessed | tf_op | source)
XLA Modules:
  0.0 51.3 jit_solution(15776616095038381543)
XLA Ops:
  0.0 50.6 %smooth_ap.1 = f32[32,1024]{1,0:T(8,128)S(1)} custom-call(bf16[32,1024]{1,0:T(8,128)(2,1)} %embed.1, s32[4,512]{1,0:T(4,128)} %bitcast.3, s32[64,128]{1,0:T(8,128)} %bitcast.2), custom_call_target="tpu_custom_call" | custom-call | flops 2147483648 | bytes 4194304 | tf_op jit(solution)/shard_map/smooth_ap/pallas_call | solution.py:503
  50.6 0.7 %copy.5 = f32[32,1024]{1,0:T(8,128)} copy(f32[32,1024]{1,0:T(8,128)S(1)} %smooth_ap.1) | data formatting | bytes 262144
